TPU v7x, 128 devices: a whole 4x4x4 slice. The times are simulated.
128 devices in a mesh: row: 16 (over z, y_hi, core), col: 8 (over y_lo, x).
Axes of the slice: x: 4, y: 4 (y_hi: 2, y_lo: 2; y = y_hi * 2 + y_lo), z: 4, core: 2. Of those that a mesh axis runs over, the one named last changes fastest.
Arguments:
- colatitude: float32 [1024], P('row'), may hold values from 0.2 to 2.94
- longitude: float32 [1024], P('row'), may hold values from -3.140625 to 3.140625
- radius_ratio: float32 [1024], P('row'), may hold values from 0.998 to 1.002
- component: int32 [1024], P('row'), may hold values from 0 to 2
- obs_weight: float32 [1024], P('row'), may hold values from 0.0009765625 to 0.015625
- observed: float32 [1024], P('row'), may hold values from -6 to 6
- unknown_map: int32 [3, 98304], replicated, may hold values from 0 to 300, as said below
- slab_map: int32 [3, 4096], P(None, 'col'), may hold values from 0 to 300, as said below
- normal_slab: float32 [98304, 4096], P('row', 'col'), may hold values from -3 to 3
- right_side: float32 [98304], P(('row', 'col')), may hold values from -6 to 6
Outputs:
- normal_out: float32 [98304, 4096], P('row', 'col')
- right_out: float32 [98304], P(('row', 'col'))
Inputs may be any that keep to these rules, and one draw needn't show every extreme that they name: `unknown_map`: row 0 is a degree, row 1 an order (at most the degree), row 2 a kind: 0 cosine, 1 sine (never for order 0), 2 an unused stored row (degree 2, order 0). The used rows hold every coefficient of degree 2 to 300 exactly once, in an order drawn from the seed. `slab_map`: rows as in unknown_map, kinds 0 or 1 only: 4096 consecutive unknowns of the order-wise numbering (order by order from 0; within an order the cosines of rising degree, then the sines), starting at a position drawn from the seed.
All inputs are finite; a program needn't handle non-finite values.
Results may differ from a plain program's by a relative error of at most 0.0003.
Values sent between devices are 32-bit elements; how exact they have to be, the bound alone decides.
A program may use at most 320 MiB of HBM per device.

v0:
```python
import jax
import jax.numpy as jnp
from jax import lax
from jax.sharding import PartitionSpec as P

N1 = 301


def legendre(colatitude):
    top = N1
    width = (top + 7) // 8 * 8
    count = colatitude.shape[0]
    cos_theta = jnp.cos(colatitude)
    sine_theta = jnp.sin(colatitude)
    order_top = jnp.arange(top).astype(jnp.float32)
    counter = jnp.arange(1, top).astype(jnp.float32)
    log_steps = 0.5 * jnp.log((2.0 * counter + 1.0) / (2.0 * counter))
    log_start = jnp.concatenate(
        [jnp.zeros((1,), jnp.float32), 0.5 * jnp.log(jnp.float32(2.0)) + jnp.cumsum(log_steps)]
    )
    log_diagonal = log_start[:, None] + order_top[:, None] * jnp.log(sine_theta)[None, :]
    log_diagonal = jnp.concatenate(
        [log_diagonal, jnp.zeros((width - top, count), jnp.float32)], axis=0
    )
    order_grid = jnp.arange(width).astype(jnp.float32)[None, :]
    degree_grid = jnp.arange(top).astype(jnp.float32)[:, None]
    denom = jnp.maximum((degree_grid - order_grid) * (degree_grid + order_grid), 1.0)
    rise_table = jnp.sqrt((2.0 * degree_grid - 1.0) * (2.0 * degree_grid + 1.0) / denom)
    fall_num = jnp.maximum(
        (2.0 * degree_grid + 1.0)
        * (degree_grid + order_grid - 1.0)
        * (degree_grid - order_grid - 1.0),
        0.0,
    )
    fall_table = jnp.sqrt(fall_num / (denom * jnp.maximum(2.0 * degree_grid - 3.0, 1.0)))
    inside_table = order_grid < degree_grid
    diagonal_table = order_grid == degree_grid
    living_table = order_grid <= degree_grid
    zeros = jnp.zeros((width, count), jnp.float32)
    cos_row = cos_theta[None, :]

    def advance(carry, tables):
        latest, earlier, log_scale = carry
        rise_coef, fall_coef, inside, diagonal_mask, living = tables
        fresh_value = rise_coef[:, None] * cos_row * latest - fall_coef[:, None] * earlier
        fresh_value = jnp.where(
            inside[:, None], fresh_value, jnp.where(diagonal_mask[:, None], 1.0, 0.0)
        )
        latest = jnp.where(inside[:, None], latest, 0.0)
        log_scale = jnp.where(diagonal_mask[:, None], log_diagonal, log_scale)
        magnitude = jnp.where(living[:, None], jnp.abs(fresh_value) + jnp.abs(latest), 1.0)
        output = fresh_value * jnp.exp(log_scale)
        return (
            (fresh_value / magnitude, latest / magnitude, log_scale + jnp.log(magnitude)),
            output,
        )

    carry_start = (zeros, zeros, zeros)
    tables = (rise_table, fall_table, inside_table, diagonal_table, living_table)
    unused, legendre_table = lax.scan(advance, carry_start, tables, unroll=4)
    return (legendre_table.reshape(top * width, count), width)


def design_rows(flat_table, width, colatitude, longitude, radius_ratio, component, index_map):
    degrees = index_map[0]
    orders = index_map[1]
    kind_flag = index_map[2]
    position = degrees * width + orders
    current = jnp.take(flat_table, position, axis=0)
    previous = jnp.take(flat_table, position - width, axis=0)
    degree_float = degrees.astype(jnp.float32)[:, None]
    order_float = orders.astype(jnp.float32)[:, None]
    cos_theta = jnp.cos(colatitude)[None, :]
    sine_theta = jnp.sin(colatitude)[None, :]
    slope_coef = jnp.sqrt(
        jnp.maximum(
            (2.0 * degree_float + 1.0) * (degree_float * degree_float - order_float * order_float),
            0.0,
        )
        / (2.0 * degree_float - 1.0)
    )
    slope = (degree_float * cos_theta * current - slope_coef * previous) / sine_theta
    radial_yy = (
        -(degree_float + 1.0) * current
        + cos_theta / sine_theta * slope
        - order_float * order_float * current / (sine_theta * sine_theta)
    ) / ((degree_float + 1.0) * (degree_float + 2.0))
    radial_xx = -current - radial_yy
    picked = component[None, :]
    component_value = jnp.where(picked == 2, current, jnp.where(picked == 1, radial_yy, radial_xx))
    attenuate = jnp.exp(-(degree_float + 3.0) * jnp.log(radius_ratio)[None, :])
    phase = order_float * longitude[None, :]
    flag = kind_flag[:, None]
    harmonic = jnp.where(flag == 0, jnp.cos(phase), jnp.where(flag == 1, jnp.sin(phase), 0.0))
    return attenuate * component_value * harmonic


def on_device(
    colatitude,
    longitude,
    radius_ratio,
    component,
    obs_weight,
    observed,
    unknown_map,
    slab_map,
    normal_slab,
    right_side,
):
    rows_count = lax.axis_size("row")
    cols_count = lax.axis_size("col")
    col_position = lax.axis_index("col")
    rows_dev = normal_slab.shape[0]
    portion = rows_dev // cols_count
    count = colatitude.shape[0]
    pair_contract = (((1,), (1,)), ((), ()))
    vector_contract = (((1,), (0,)), ((), ()))
    flat_table, width = legendre(colatitude)
    grouped = unknown_map.reshape(3, rows_count, cols_count, portion)
    chosen = lax.dynamic_index_in_dim(grouped, col_position, axis=2, keepdims=False).reshape(
        3, rows_count * portion
    )
    built = design_rows(flat_table, width, colatitude, longitude, radius_ratio, component, chosen)
    built = built.reshape(rows_count, portion, count)
    weighted = (
        design_rows(flat_table, width, colatitude, longitude, radius_ratio, component, slab_map)
        * obs_weight[None, :]
    )
    scaled = obs_weight * observed
    slab_all, scaled_all = (
        lax.all_gather(weighted, "row", axis=1, tiled=True),
        lax.all_gather(scaled, "row", axis=0, tiled=True),
    )
    relayed = lax.all_to_all(built, "row", split_axis=0, concat_axis=2, tiled=True)
    relayed = relayed.reshape(portion, relayed.shape[2])
    right_out = right_side + lax.dot_general(
        relayed, scaled_all, vector_contract, precision=lax.Precision.HIGHEST
    )
    update = lax.dot_general(
        lax.all_gather(relayed, "col", axis=0, tiled=True),
        slab_all,
        pair_contract,
        precision=lax.Precision.HIGHEST,
    )
    return (normal_slab + update, right_out)


def solution(mesh):
    return jax.shard_map(
        on_device,
        mesh=mesh,
        in_specs=(
            P("row"),
            P("row"),
            P("row"),
            P("row"),
            P("row"),
            P("row"),
            P(),
            P(None, "col"),
            P("row", "col"),
            P(("row", "col")),
        ),
        out_specs=(P("row", "col"), P(("row", "col"))),
        check_vma=False,
    )
```

profile of v0, /device:TPU:1, one launch (start us, length us, event | category | flops | bytes accessed | tf_op | source)
XLA Modules:
  0.0 834.0 jit_solution(9649054957055303747)
XLA Ops:
  13.4 235.9 %while.17 = (s32[]{:T(128)}, f32[304,64]{1,0:T(8,128)S(1)}, f32[304,64]{1,0:T(8,128)S(1)}, f32[304,64]{1,0:T(8,128)S(1)}, f32[75,4,304,64]{3,2,1,0:T(8,128)}, /*...) while((s32[]{:T(128)}, f32[304,64]{1,0:T(8,128)S(1)}, ...), condition=%wide.region_3.4_spmd.clone, body=%wide.region_2.3_spmd.clone.sunk | while | flops 1771718 | bytes 3404008 | solution.py:60
  22.0 0.9 fusion.60
  56.5 0.9 fusion.60
  59.7 0.9 fusion.60
  78.6 0.9 fusion.60
  81.7 0.9 fusion.60
  94.3 0.9 fusion.60
  106.9 0.9 fusion.60
  113.2 0.9 fusion.60
  141.4 0.9 fusion.60
  144.6 1.0 fusion.60
  163.5 0.9 fusion.60
  166.7 0.9 fusion.60
  185.5 0.9 fusion.60
  188.7 0.9 fusion.60
  204.4 0.9 fusion.60
  210.7 0.9 fusion.60
  217.0 0.9 fusion.60
  226.4 0.9 fusion.60
  235.9 0.9 fusion.60
  249.6 34.3 %pad_maximum_fusion = f32[301,304,64]{2,1,0:T(8,128)} fusion(f32[1,304,64]{2,1,0:T(8,128)S(1)} %multiply_bitcast_fusion.4, f32[300,304,64]{2,1,0:T(8,128)} %bitcast.81), kind=kLoop, calls=%fused_computation.61 | loop fusion | flops 5856256 | bytes 46850048 | tf_op jit(solution)/shard_map/concatenate | solution.py:60
  283.9 15.5 %gather_fusion.3 = f32[512,64]{1,0:T(8,128)S(1)} fusion(f32[91504,64]{1,0:T(8,128)} %bitcast.77, s32[1024]{0:T(1024)S(1)} %get-tuple-element.224), kind=kCustom, calls=%fused_computation.3.clone | custom fusion | bytes 264192 | tf_op jit(solution)/shard_map/jit(_take)/gather | solution.py:70
  299.5 15.4 %gather_fusion.2 = f32[512,64]{1,0:T(8,128)S(1)} fusion(f32[91504,64]{1,0:T(8,128)} %bitcast.78, s32[1024]{0:T(1024)S(1)} %get-tuple-element.225), kind=kCustom, calls=%fused_computation.1.clone | custom fusion | bytes 264192 | tf_op jit(solution)/shard_map/jit(_take)/gather | solution.py:69
  315.1 1.3 fusion.35
  317.2 55.9 %gather_fusion.1 = f32[12288,64]{1,0:T(8,128)} fusion(f32[91504,64]{1,0:T(8,128)} %bitcast.79, s32[12288]{0:T(1024)S(1)} %get-tuple-element.196), kind=kCustom, calls=%fused_computation.2.clone | custom fusion | bytes 6340608 | tf_op jit(solution)/shard_map/jit(_take)/gather | solution.py:70
  373.1 55.5 %gather_fusion = f32[12288,64]{1,0:T(8,128)} fusion(f32[91504,64]{1,0:T(8,128)} %bitcast.80, s32[12288]{0:T(1024)S(1)} %get-tuple-element.195), kind=kCustom, calls=%fused_computation.clone | custom fusion | bytes 6340608 | tf_op jit(solution)/shard_map/jit(_take)/gather | solution.py:69
  428.6 34.6 %fusion.14 = f32[12288,64]{1,0:T(8,128)} fusion(f32[12288,64]{1,0:T(8,128)} %gather_fusion.1, f32[12288,64]{1,0:T(8,128)} %gather_fusion, f32[64]{0:T(128)S(1)} %copy-done.2, f32[12288]{0:T(1024)S(1)} %convert_element_type.147, f32[12288]{0:T(1024)S(1)} %get-tuple-element.191, f32[64]{0:T(128)S(1)} %get-tuple-element.214, f32[12288]{0:T(1024)S(1)} %get-tuple-element.184, ...), kind=kLoop, calls=%fused_computation.67 | loop fusion | flops 18874368 | bytes 9832064 | tf_op jit(solution)/shard_map/mul | solution.py:95
  463.2 4.4 copy.18
  467.7 48.9 %all_to_all.15 = f32[16,768,64]{1,2,0:T(8,128)} all-to-all(f32[16,768,64]{1,2,0:T(8,128)S(1)} %copy.18), channel_id=1, replica_groups=mesh['row'=16,'col'=8] {'row'}, dimensions={0} | all-to-all | bytes 6291456 | tf_op jit(solution)/shard_map/all_to_all | solution.py:134
  518.0 259.8 %all-reduce.2 = f32[1024]{0:T(1024)S(1)} all-reduce(f32[1024]{0:T(1024)S(1)} %multiply_dynamic-update-slice_fusion), channel_id=1, replica_groups=mesh['row'=16,'col'=8] {'row'}, use_global_device_ids=true, to_apply=%add.2 | all-reduce | flops 1024 | bytes 8192
  777.8 3.6 convolution_reduce_fusion
  782.0 45.1 %convolution_add_fusion = f32[6144,512]{1,0:T(8,128)} fusion(f32[6144,512]{1,0:T(8,128)} %param.24, f32[6144,1024]{0,1:T(8,128)} %all-gather.3.cloned.1.call-done, f32[512,1024]{0,1:T(8,128)} %all-gather.5.cloned.1.call-done), kind=kOutput, calls=%fused_computation.65 | convolution fusion | flops 38657851392 | bytes 52428800 | tf_op jit(solution)/shard_map/dot_general | solution.py:139
  (959 shorter events, 222.1 us)
Async XLA Ops:
  7.2 774.9 %all-gather.5.cloned.1.call-start = ((), (), s32[]{:S(2)}) async-start(), calls=%async_computation.2 | async-start | bytes 2228224 | tf_op jit(solution)/shard_map/all_gather | solution.py:131
  249.6 65.5 %copy-start.2 = (f32[64]{0:T(128)S(1)}, f32[64]{0:T(128)}, u32[]{:S(2)}) copy-start(f32[64]{0:T(128)} %param.17) | copy-start | bytes 772
  249.6 65.5 %copy-start.3 = (f32[64]{0:T(128)S(1)}, f32[64]{0:T(128)}, u32[]{:S(2)}) copy-start(f32[64]{0:T(128)} %param.20) | copy-start | bytes 772
  283.9 32.6 %copy-start = (s32[3,98304]{1,0:T(4,128)S(1)}, s32[3,98304]{1,0:T(4,128)}, u32[]{:S(2)}) copy-start(s32[3,98304]{1,0:T(4,128)} %param.22) | copy-start | bytes 3538948
  316.5 465.5 %all-gather.3.cloned.1.call-start = ((), (), s32[]{:S(2)}) async-start(), calls=%async_computation.1 | async-start | bytes 28311552 | tf_op jit(solution)/shard_map/all_gather | solution.py:140
  467.7 49.0 %copy-start.5 = (u32[128]{0:T(128)S(1)}, u32[128]{0:T(128)}, u32[]{:S(2)}) copy-start(u32[128]{0:T(128)} %constant.70) | copy-start | bytes 1540
  467.7 50.2 %copy-start.4 = (f32[64]{0:T(128)S(1)}, f32[64]{0:T(128)}, u32[]{:S(2)}) copy-start(f32[64]{0:T(128)} %param.21) | copy-start | bytes 772
  467.7 313.7 %copy-start.1 = (f32[768]{0:T(1024)S(1)}, f32[768]{0:T(1024)}, u32[]{:S(2)}) copy-start(f32[768]{0:T(1024)} %param.25) | copy-start | bytes 9220
Sparse Core Ops, SparseCore 0:
  316.6 51.2 all-gather.4
  516.7 246.3 all-gather.2
where the time goes:
time: 840 us; the launch traced here: 834 us
  blocking collectives  309 us (37%)
  other arithmetic  294 us (35%)
  local copies, waits for them, and re-layouts  162 us (19%)
  matrix products  48.7 us (6%)
  between operations  15.1 us (2%)
    unnamed x1, blocking collectives  260 us
    broadcast_in_dim x227, other arithmetic, legendre(): unused, legendre_table = lax.scan(advance, carry_start, tables, unroll=4)  140 us
    gather x3, local copies, waits for them, and re-layouts, design_rows(): previous = jnp.take(flat_table, position - width, axis=0)  71.5 us
    gather x3, local copies, waits for them, and re-layouts, design_rows(): current = jnp.take(flat_table, position, axis=0)  71 us
    dynamic_update_slice x75, other arithmetic, legendre(): unused, legendre_table = lax.scan(advance, carry_start, tables, unroll=4)  66.7 us
    all_to_all x1, blocking collectives, on_device(): lax.all_to_all(built, 'row', split_axis=0, concat_axis=2, tiled=True)  48.9 us
    dot_general x1, matrix products, on_device(): lax.dot_general(lax.all_gather(relayed, 'col', axis=0, tiled=True), slab_...  45.1 us
    mul x1, other arithmetic, design_rows(): return attenuate * component_value * harmonic  34.6 us
  transfers between devices with their start and end apart: 2, of which 0 were waited for; matrix products, arithmetic and copies ran while one was open for 19% of the time, Pallas kernels for 0%

commit v1 on v0

v1 whole, which is shorter than its diff:
```python
import jax
import jax.numpy as jnp
import numpy as np
from jax import lax
from jax.experimental import pallas as pl
from jax.experimental.pallas import tpu as pltpu
from jax.sharding import PartitionSpec as P

NMAX = 300
TOP = 304
GROUP = 8
GROUPS = TOP // GROUP
STEP = 16
SLOT = STEP + 1
BLOCKS = (NMAX + STEP) // STEP
OBS = 1024
PARTS = 8
UNROLL = 8
CHUNK = 256
SPARE = 310
BASE = 256
BIG = float(2.0**64)
SMALL = float(2.0**-64)
LOG_BIG = float(64.0 * np.log(2.0))
F32 = jnp.float32
BF16 = jnp.bfloat16


def diagonal_logs():
    counter = np.arange(1, TOP, dtype=np.float64)
    steps = 0.5 * np.log((2.0 * counter + 1.0) / (2.0 * counter))
    logs = np.concatenate([[0.0], 0.5 * np.log(2.0) + np.cumsum(steps)])
    return np.broadcast_to(logs[:, None], (TOP, 128)).astype(np.float32)


def inverse_squares():
    degree = np.arange(TOP + 2 * STEP, dtype=np.float64)
    return (1.0 / (degree * degree - 0.25)).astype(np.float32)


def row_facts(degree, order, kind):
    group = order // GROUP
    offset = degree - group * GROUP
    block = offset // STEP
    lane = order % GROUP
    at_value = (block * SLOT + 1 + offset % STEP) * 64 + lane
    at_scale = block * 64 + lane
    n = degree.astype(F32)
    m = order.astype(F32)
    first = group * GROUP + block * STEP
    upto = jnp.ones_like(n)
    before = jnp.ones_like(n)
    for q in range(STEP):
        j = first + q
        jf = j.astype(F32)
        ratio = jnp.where(j > order, (jf * jf - m * m) / (jf * jf - 0.25), 1.0)
        upto = jnp.where(j <= degree, upto * ratio, upto)
        before = jnp.where(j < degree, before * ratio, before)
    grow = lax.rsqrt(upto)
    grow_before = lax.rsqrt(before)
    denom = (n + 1.0) * (n + 2.0)
    mix = grow * (n - m * m) / denom
    slope = jnp.sqrt(jnp.maximum((2.0 * n + 1.0) * (n * n - m * m), 0.0) / (2.0 * n - 1.0))
    past = -grow_before * slope / denom
    return at_value, at_scale, degree * 2, order * 2 + kind, grow, mix, past


def group_starts(order):
    bounds = jnp.arange(GROUPS + 1, dtype=jnp.int32) * GROUP
    return jnp.sum((order[None, :] < bounds[:, None]).astype(jnp.int32), axis=1)


def kernel(
    col_ref, starts_ref, slab_starts_ref, inv_ref,
    rv_ref, rs_ref, rn_ref, rh_ref, rg_ref, rm_ref, rp_ref, rd_ref,
    sv_ref, ss_ref, sn_ref, sh_ref, sg_ref, sm_ref, sp_ref,
    params_ref, logs_ref, right_ref, normal_ref,
    out_ref, right_out_ref,
    value_buf, scale_buf, harm_buf, radial_buf, design_buf, slab_buf,
    slab_hi, slab_lo, in_buf, out_buf, in_sem, out_sem,
):
    rows = normal_ref.shape[0]
    chunks = rows // CHUNK

    def fetch(index, slot):
        return pltpu.make_async_copy(
            normal_ref.at[pl.ds(pl.multiple_of(index * CHUNK, CHUNK), CHUNK)], in_buf.at[slot], in_sem.at[slot]
        )

    def put(index, slot):
        return pltpu.make_async_copy(
            out_buf.at[slot], out_ref.at[pl.ds(pl.multiple_of(index * CHUNK, CHUNK), CHUNK)], out_sem.at[slot]
        )

    fetch(0, 0).start()
    fetch(1, 1).start()

    theta = params_ref[0]
    lon = params_ref[1]
    cos_t = jnp.cos(theta)
    sin_t = jnp.sin(theta)
    log_s = jnp.log(sin_t)
    comp = params_ref[3]
    weight = params_ref[4]
    scaled = weight * params_ref[5]
    part0 = jnp.where(comp == 2.0, 1.0, jnp.where(comp == 1.0, 0.0, -1.0))
    part1 = jnp.where(comp == 2.0, 0.0, jnp.where(comp == 1.0, 1.0, -1.0))
    part1q = part1 / (sin_t * sin_t)
    inv_r = 1.0 / params_ref[2]

    c1 = jnp.cos(lon)
    s1 = jnp.sin(lon)
    cs = [jnp.ones_like(c1)]
    sn = [jnp.zeros_like(c1)]
    for _ in range(8):
        cs.append(cs[-1] * c1 - sn[-1] * s1)
        sn.append(sn[-1] * c1 + cs[-2] * s1)
    c8, s8 = cs[8], sn[8]
    powers = [inv_r * inv_r * inv_r]
    step_r = inv_r
    for _ in range(7):
        powers.append(powers[-1] * inv_r)
    for _ in range(3):
        step_r = step_r * step_r

    def fill(block, carry):
        cc, ss, pw = carry
        base = block * 8
        for j in range(8):
            harm_buf[(base + j) * 2] = cc[j]
            harm_buf[(base + j) * 2 + 1] = ss[j]
            nf = (base + j).astype(F32)
            ratio = (2.0 * nf + 1.0) / ((nf + 1.0) * (nf + 2.0))
            radial_buf[(base + j) * 2] = pw[j] * (part0 - part1 * ratio)
            radial_buf[(base + j) * 2 + 1] = pw[j] * part1q
        return (
            tuple(cc[j] * c8 - ss[j] * s8 for j in range(8)),
            tuple(ss[j] * c8 + cc[j] * s8 for j in range(8)),
            tuple(pw[j] * step_r for j in range(8)),
        )

    lax.fori_loop(0, TOP // 8, fill, (tuple(cs[:8]), tuple(sn[:8]), tuple(powers)))

    sub = lax.broadcasted_iota(jnp.int32, (8, 128), 0)
    subf = sub.astype(F32)

    def spread(values, c):
        return jnp.broadcast_to(values[c : c + 1, :], (8, 128))

    twice = [spread(2.0 * cos_t, c) for c in range(PARTS)]
    logs = [spread(log_s, c) for c in range(PARTS)]

    def entry(v_ref, s_ref, n_ref, h_ref, g_ref, m_ref, p_ref, j):
        at = v_ref[j]
        now = value_buf[pl.ds(at, 8, stride=8), :]
        past = value_buf[pl.ds(at - 64, 8, stride=8), :]
        scale = scale_buf[pl.ds(s_ref[j], 8, stride=8), :]
        f = radial_buf[n_ref[j]]
        g = radial_buf[n_ref[j] + 1]
        h = harm_buf[h_ref[j]]
        body = now * (g_ref[j] * f + m_ref[j] * g) + (p_ref[j] * past) * (cos_t * g)
        return (h * scale) * body

    def group_body(group, _):
        first = group * GROUP
        orders = subf + first.astype(F32)
        squares = orders * orders
        orders_i = sub + first
        diag = logs_ref[pl.ds(pl.multiple_of(first, 8), 8), :]

        def put_values(slot, values):
            at = pl.multiple_of(slot * 64, 64)
            value_buf[pl.ds(at, 64), :] = jnp.concatenate(values, axis=0)

        def ratio_at(j):
            jf = j.astype(F32)
            return (jf * jf - squares) * inv_ref[j]

        seeds = []
        levels = []
        scales = []
        for c in range(PARTS):
            log_seed = diag + orders * logs[c]
            level = jnp.minimum(jnp.ceil(log_seed * (1.0 / LOG_BIG)), 0.0)
            seeds.append(jnp.exp(log_seed - level * LOG_BIG))
            levels.append(level)
            scales.append(jnp.where(level >= 0.0, 1.0, jnp.where(level >= -1.0, SMALL, 0.0)))
        scale_buf[pl.ds(0, 64), :] = jnp.concatenate(scales, axis=0)
        zero = jnp.zeros((8, 128), F32)
        one = [zero] * PARTS
        two = [zero] * PARTS
        put_values(0, one)
        total = jnp.ones((8, 128), F32)
        rho = ratio_at(jnp.maximum(first - 1, 0))
        for i in range(STEP):
            fresh = [twice[c] * one[c] - rho * two[c] for c in range(PARTS)]
            if i < GROUP:
                fresh = [jnp.where(sub == i, seeds[c], fresh[c]) for c in range(PARTS)]
            put_values(1 + i, fresh)
            one, two = fresh, one
            rho = ratio_at(first + i)
            total = total * jnp.where(orders_i < first + i, rho, 1.0)

        def block_body(block, carry):
            one, two, levels, total, rho = carry
            start = first + block * STEP
            sigma = lax.rsqrt(total)
            sigma_small = sigma * SMALL
            limit = 64.0 * total * sigma
            scales = []
            one, two, levels = list(one), list(two), list(levels)
            for c in range(PARTS):
                big = jnp.abs(one[c]) > limit
                factor = jnp.where(big, sigma_small, sigma)
                one[c] = one[c] * factor
                two[c] = two[c] * factor
                levels[c] = jnp.where(big, levels[c] + 1.0, levels[c])
                scales.append(
                    jnp.where(levels[c] >= 0.0, 1.0, jnp.where(levels[c] >= -1.0, SMALL, 0.0))
                )
            scale_buf[pl.ds(pl.multiple_of(block * 64, 64), 64), :] = jnp.concatenate(scales, axis=0)
            put_values(block * SLOT, one)
            total = jnp.ones((8, 128), F32)
            for i in range(STEP):
                fresh = [twice[c] * one[c] - rho * two[c] for c in range(PARTS)]
                put_values(block * SLOT + 1 + i, fresh)
                one, two = fresh, one
                rho = ratio_at(start + i)
                total = total * rho
            return tuple(one), tuple(two), tuple(levels), total, rho

        blocks = (NMAX + 1 - first + STEP - 1) // STEP
        lax.fori_loop(1, blocks, block_body, (tuple(one), tuple(two), tuple(levels), total, rho))

        def slab_rows(piece, _):
            for u in range(UNROLL):
                j = slab_starts_ref[group] + piece * UNROLL + u
                value = entry(sv_ref, ss_ref, sn_ref, sh_ref, sg_ref, sm_ref, sp_ref, j)
                slab_buf[pl.ds((j // 8) * 64 + j % 8, 8, stride=8), :] = value * weight
            return 0

        count = slab_starts_ref[group + 1] - slab_starts_ref[group]
        lax.fori_loop(0, (count + UNROLL - 1) // UNROLL, slab_rows, 0)

        def main_rows(piece, _):
            for u in range(UNROLL):
                j = starts_ref[group] + piece * UNROLL + u
                value = entry(rv_ref, rs_ref, rn_ref, rh_ref, rg_ref, rm_ref, rp_ref, j)
                design_buf[pl.ds(rd_ref[j], 8, stride=8), :] = value
            return 0

        count = starts_ref[group + 1] - starts_ref[group]
        lax.fori_loop(0, (count + UNROLL - 1) // UNROLL, main_rows, 0)
        return 0

    lax.fori_loop(0, GROUPS, group_body, 0)

    def clear(j, _):
        design_buf[pl.ds(rd_ref[j], 8, stride=8), :] = jnp.zeros((8, 128), F32)
        return 0

    lax.fori_loop(starts_ref[GROUPS], rows, clear, 0)

    slab_view = slab_buf.reshape(slab_buf.shape[0] // 64, 8, 8, 128)
    width = out_ref.shape[1]
    for c in range(PARTS):
        for half in range(width // 256):
            block = slab_view[pl.ds(half * 32, 32), c].reshape(256, 128).T
            hi = block.astype(BF16)
            slab_hi[pl.ds(c * 128, 128), pl.ds(half * 256, 256)] = hi
            slab_lo[pl.ds(c * 128, 128), pl.ds(half * 256, 256)] = (block - hi.astype(F32)).astype(BF16)

    view = design_buf.reshape(design_buf.shape[0] // 64, 8, 8, 128)

    own = right_ref.shape[1]
    total = jnp.zeros((own, 128), F32)
    at = col_ref[0] * (own // 8)
    for c in range(PARTS):
        total = total + view[pl.ds(at, own // 8), c].reshape(own, 128) * scaled[c : c + 1, :]
    summed = lax.dot_general(
        jnp.ones((8, 128), F32), total, (((1,), (1,)), ((), ())),
        precision=lax.Precision.HIGHEST, preferred_element_type=F32,
    )
    right_out_ref[...] = right_ref[...] + summed[0:1, :]

    def chunk_body(index, _):
        slot = lax.rem(index, 2)
        his = []
        los = []
        for c in range(PARTS):
            x = view[pl.ds(index * (CHUNK // 8), CHUNK // 8), c].reshape(CHUNK, 128)
            hi = x.astype(BF16)
            his.append(hi)
            los.append((x - hi.astype(F32)).astype(BF16))
        hi = jnp.concatenate(his, axis=1)
        lo = jnp.concatenate(los, axis=1)
        update = jnp.dot(hi, slab_hi[...], preferred_element_type=F32)
        update += jnp.dot(hi, slab_lo[...], preferred_element_type=F32)
        update += jnp.dot(lo, slab_hi[...], preferred_element_type=F32)
        fetch(index, slot).wait()

        @pl.when(index >= 2)
        def _():
            put(index - 2, slot).wait()

        out_buf[slot] = in_buf[slot] + update
        put(index, slot).start()

        @pl.when(index + 2 < chunks)
        def _():
            fetch(index + 2, slot).start()

        return 0

    lax.fori_loop(0, chunks, chunk_body, 0)
    put(chunks - 2, 0).wait()
    put(chunks - 1, 1).wait()


def local_update(params, col, unknowns, slab_map, normal_slab, right_side):
    rows, width = normal_slab.shape
    own = right_side.shape[0]
    degree, order, kind = unknowns[0], unknowns[1], unknowns[2]
    place = lax.broadcasted_iota(jnp.int32, (rows,), 0)
    unused = kind == 2
    key = (
        ((jnp.where(unused, SPARE, order) - BASE) << 23)
        | (degree << 14)
        | (jnp.where(unused, 0, kind) << 13)
        | place
    )
    key = lax.sort(key, is_stable=False)
    order = (key >> 23) + BASE
    starts = group_starts(order)
    unused = order > NMAX
    order = jnp.where(unused, 0, order)
    degree = (key >> 14) & 511
    kind = (key >> 13) & 1
    place = key & 8191
    target = (place // 8) * 64 + place % 8
    facts = row_facts(degree, order, kind)
    pad = UNROLL
    facts = tuple(jnp.concatenate([x, x[:1] + jnp.zeros((pad,), x.dtype)]) for x in facts)
    target = jnp.concatenate([target, (rows // 8) * 64 + jnp.arange(pad, dtype=jnp.int32)])
    slab_facts = row_facts(slab_map[0], slab_map[1], slab_map[2])
    slab_facts = tuple(jnp.concatenate([x, x[:1] + jnp.zeros((pad,), x.dtype)]) for x in slab_facts)
    slab_starts = group_starts(slab_map[1])

    smem = pl.BlockSpec(memory_space=pltpu.SMEM)
    vmem = pl.BlockSpec(memory_space=pltpu.VMEM)
    hbm = pl.BlockSpec(memory_space=pltpu.HBM)
    out, right = pl.pallas_call(
        kernel,
        out_shape=(
            jax.ShapeDtypeStruct((rows, width), F32),
            jax.ShapeDtypeStruct((1, own), F32),
        ),
        in_specs=[smem] * 19 + [vmem] * 3 + [hbm],
        out_specs=(hbm, vmem),
        scratch_shapes=[
            pltpu.VMEM((BLOCKS * SLOT * 64, 128), F32),
            pltpu.VMEM((BLOCKS * 64, 128), F32),
            pltpu.VMEM((TOP * 2, 8, 128), F32),
            pltpu.VMEM((TOP * 2, 8, 128), F32),
            pltpu.VMEM(((rows // 8 + 1) * 64, 128), F32),
            pltpu.VMEM(((width // 8 + 1) * 64, 128), F32),
            pltpu.VMEM((OBS, width), BF16),
            pltpu.VMEM((OBS, width), BF16),
            pltpu.VMEM((2, CHUNK, width), F32),
            pltpu.VMEM((2, CHUNK, width), F32),
            pltpu.SemaphoreType.DMA((2,)),
            pltpu.SemaphoreType.DMA((2,)),
        ],
        compiler_params=pltpu.CompilerParams(vmem_limit_bytes=60 * 1024 * 1024),
        name="normal_update",
    )(
        col, starts, slab_starts, jnp.asarray(inverse_squares()),
        *facts, target, *slab_facts,
        params, jnp.asarray(diagonal_logs()), right_side.reshape(1, own), normal_slab,
    )
    return out, right.reshape(own)


def on_device(
    colatitude, longitude, radius_ratio, component, obs_weight, observed,
    unknown_map, slab_map, normal_slab, right_side,
):
    zeros = jnp.zeros_like(colatitude)
    local = jnp.stack(
        [colatitude, longitude, radius_ratio, component.astype(F32), obs_weight, observed, zeros, zeros]
    )
    params = lax.all_gather(local, "row", axis=0)
    params = params.transpose(1, 0, 2).reshape(8, PARTS, 128)
    rows = normal_slab.shape[0]
    unknowns = lax.dynamic_slice_in_dim(unknown_map, lax.axis_index("row") * rows, rows, axis=1)
    col = lax.axis_index("col").astype(jnp.int32).reshape(1)
    return local_update(params, col, unknowns, slab_map, normal_slab, right_side)


def solution(mesh):
    return jax.shard_map(
        on_device,
        mesh=mesh,
        in_specs=(
            P("row"), P("row"), P("row"), P("row"), P("row"), P("row"),
            P(), P(None, "col"), P("row", "col"), P(("row", "col")),
        ),
        out_specs=(P("row", "col"), P(("row", "col"))),
        check_vma=False,
    )
```

time: 840 us -> 187 us (0.22)
  other arithmetic: 294 us -> 11.4 us
  blocking collectives: 309 us -> 27.2 us
  local copies, waits for them, and re-layouts: 162 us -> 27.9 us
  Pallas kernels: 0 us -> 120 us
  matrix products: 48.7 us -> 0 us
  between operations: 15.1 us -> 0.69 us
    unnamed x1 -> x0, blocking collectives: 260 us -> none
    gather x6 -> x0, local copies, waits for them, and re-layouts: 142 us -> none  [the longest x3 71.5 us: design_rows(): previous = jnp.take(flat_table, position - width, axis=0)]
    broadcast_in_dim x227 -> x0, other arithmetic: 140 us -> none  [legendre(): unused, legendre_table = lax.scan(advance, carry_start, tables, unroll=4)]
    pallas_call x0 -> x1, Pallas kernels: none -> 120 us  [local_update(): pl.pallas_call(kernel, out_shape=(jax.ShapeDtypeStruct((rows, width), F32...]
    dynamic_update_slice x75 -> x0, other arithmetic: 66.7 us -> none  [legendre(): unused, legendre_table = lax.scan(advance, carry_start, tables, unroll=4)]
    all_to_all x1 -> x0, blocking collectives: 48.9 us -> none  [on_device(): lax.all_to_all(built, 'row', split_axis=0, concat_axis=2, tiled=True)]
    dot_general x2 -> x0, matrix products: 48.7 us -> none  [the longest x1 45.1 us: on_device(): lax.dot_general(lax.all_gather(relayed, 'col', axis=0, tiled=True), slab_...]
    mul x4 -> x1, other arithmetic: 36 us -> 0.01 us  [group_starts(): bounds = jnp.arange(GROUPS + 1, dtype=jnp.int32) * GROUP]
  transfers between devices with their start and end apart: 2 -> 0, of which waited for: 0 -> 0; matrix products, arithmetic and copies ran while one was open for 19% -> 0% of each run, Pallas kernels for 0% -> 0%
where the time goes in v1:
time: 187 us
  Pallas kernels  120 us (64%)
  local copies, waits for them, and re-layouts  27.9 us (15%)
  blocking collectives  27.2 us (15%)
  other arithmetic  11.4 us (6%)
    pallas_call x1, Pallas kernels, local_update(): pl.pallas_call(kernel, out_shape=(jax.ShapeDtypeStruct((rows, width), F32...  120 us
    all_gather x1, blocking collectives, on_device(): params = lax.all_gather(local, 'row', axis=0)  27.2 us
    concatenate x14, local copies, waits for them, and re-layouts, local_update(): jnp.concatenate([x, x[:1] + jnp.zeros((pad,), x.dtype)])  17.1 us
    slice x14, local copies, waits for them, and re-layouts, local_update(): x[:1] + jnp.zeros((pad,), x.dtype)  7.35 us
    sort x1, other arithmetic, local_update(): key = lax.sort(key, is_stable=False)  5.58 us

profile of v1, /device:TPU:1, one launch (start us, length us, event | category | flops | bytes accessed | tf_op | source)
XLA Modules:
  0.0 187.0 jit_solution(15546889817242139294)
XLA Ops:
  0.6 0.7 convert_bitcast_fusion
  1.3 0.7 stack.31
  2.1 1.3 reshape.25.right_ref
  3.3 0.8 fusion.55
  4.1 0.7 convert_reduce_fusion.1.slab_starts_ref
  5.4 1.2 concatenate.59.sp_ref
  6.7 0.5 slice.78
  7.8 0.5 slice.77
  9.9 1.2 concatenate.54.ss_ref
  11.1 1.2 concatenate.58.sm_ref
  12.3 1.2 concatenate.53.sv_ref
  13.5 1.2 concatenate.55.sn_ref
  14.7 1.2 concatenate.56.sh_ref
  15.9 1.2 concatenate.57.sg_ref
  17.1 27.2 %all-gather = f32[128,64]{1,0:T(8,128)S(1)} all-gather(f32[8,64]{1,0:T(8,128)S(1)} %stack.31), channel_id=2, replica_groups=mesh['row'=16,'col'=8] {'row'}, dimensions={0}, use_global_device_ids=true | all-gather | bytes 34816 | tf_op jit(solution)/shard_map/all_gather | solution.py:392
  44.3 0.7 reshape.24.params_ref
  45.0 1.2 fusion.54
  46.3 5.6 %sort.7 = s32[6144]{0:T(1024)S(1)} sort(s32[6144]{0:T(1024)S(1)} %fusion.4), dimensions={0}, to_apply=%region_0.1 | sort | flops 79872 | bytes 49152 | tf_op jit(solution)/shard_map/sort | solution.py:332
  52.1 0.5 slice.87
  53.2 0.5 slice.86
  53.7 1.2 concatenate.50.rm_ref
  54.9 1.2 concatenate.49.rg_ref
  56.2 1.2 concatenate.51.rp_ref
  59.0 0.6 slice.83
  59.6 0.9 convert_reduce_fusion.starts_ref
  60.5 0.6 pad_add_fusion.rd_ref
  61.1 1.2 concatenate.47.rn_ref
  62.3 1.2 concatenate.46.rs_ref
  63.5 1.2 concatenate.48.rh_ref
  64.7 1.2 concatenate.45.rv_ref
  65.9 119.7 %normal_update.1 = (f32[6144,512]{1,0:T(8,128)}, f32[1,768]{1,0:T(1,128)}) custom-call(s32[1]{0:T(128)} %bitcast.col_ref, s32[39]{0:T(128)} %convert_reduce_fusion.starts_ref, s32[39]{0:T(128)} %convert_reduce_fusion.1.slab_starts_ref, f32[336]{0:T(512)} %constant.220.clone.inv_ref, s32[6152]{0:T(1024)} %concatenate.45.rv_ref, s32[6152]{0:T(1024)} %concatenate.46.rs_ref, ...), custom_call_target="tpu_custom_call" | custom-call | tf_op jit(solution)/shard_map/normal_update/pallas_call | solution.py:352
  185.7 1.3 reduce
  (19 shorter events, 5.2 us)

commit v2 on v1

v2 whole, which is shorter than its diff:
```python
import jax
import jax.numpy as jnp
import numpy as np
from jax import lax
from jax.experimental import pallas as pl
from jax.experimental.pallas import tpu as pltpu
from jax.sharding import PartitionSpec as P

NMAX = 300
TOP = 304
GROUP = 8
GROUPS = TOP // GROUP
STEP = 16
SLOT = STEP + 1
PITCH = 9
WIDE = 8 * PITCH
RING = 8
BUFS = 4
OBS = 1024
PARTS = 8
CHUNK = 256
DRAIN = 8
LATE = 1 << 20
BIG = float(2.0**64)
SMALL = float(2.0**-64)
LOG_BIG = float(64.0 * np.log(2.0))
F32 = jnp.float32
BF16 = jnp.bfloat16
I32 = jnp.int32


def blocks_of(group):
    return (NMAX + STEP - group * GROUP) // STEP


def diagonal_logs():
    counter = np.arange(1, TOP, dtype=np.float64)
    steps = 0.5 * np.log((2.0 * counter + 1.0) / (2.0 * counter))
    logs = np.concatenate([[0.0], 0.5 * np.log(2.0) + np.cumsum(steps)])
    return np.broadcast_to(logs[:, None], (TOP, 128)).astype(np.float32)


def block_scales():
    table = []
    for group in range(GROUPS):
        order = (group * GROUP + np.arange(GROUP, dtype=np.float64))[:, None]
        for block in range(blocks_of(group)):
            sigma = np.ones((GROUP, 1))
            if block > 0:
                degree = order + STEP * (block - 1) + np.arange(STEP)[None, :]
                ratio = (degree**2 - order**2) / (degree**2 - 0.25)
                if block == 1:
                    ratio[:, 0] = 1.0
                sigma = 1.0 / np.sqrt(np.prod(ratio, axis=1, keepdims=True))
            table.append(np.broadcast_to(sigma, (GROUP, 128)))
    table.append(np.ones((GROUP, 128)))
    return np.concatenate(table, axis=0).astype(np.float32)


def inverse_squares():
    degree = np.arange(TOP + 2 * STEP, dtype=np.float64)[:, None] - 1.0
    return np.broadcast_to(1.0 / (degree * degree - 0.25), (TOP + 2 * STEP, 128)).astype(np.float32)


BLOCKS = sum(blocks_of(group) for group in range(GROUPS))


def list_keys(unknowns, slab_map):
    rows = unknowns.shape[1]
    width = slab_map.shape[1]
    total = -(-(rows + width + 64) // 1024) * 1024
    degree = jnp.concatenate([unknowns[0], slab_map[0], jnp.full((total - rows - width,), 2, I32)])
    order = jnp.concatenate([unknowns[1], slab_map[1], jnp.zeros((total - rows - width,), I32)])
    kind = jnp.concatenate([unknowns[2], slab_map[2], jnp.full((total - rows - width,), 2, I32)])
    place = lax.broadcasted_iota(I32, (total,), 0)
    beyond = degree - order
    key = (
        (((order >> 3) - 32) << 26)
        | ((beyond >> 4) << 21)
        | ((beyond & 15) << 17)
        | ((order & 7) << 14)
        | (kind << 13)
        | place
    )
    return jnp.where(kind == 2, (31 << 26) | place, key)


def list_facts(key, limit):
    group = (key >> 26) + 32
    used = group < GROUPS
    group = jnp.where(used, group, 0)
    block = jnp.where(used, (key >> 21) & 31, 0)
    step = jnp.where(used, (key >> 17) & 15, 2)
    lane = jnp.where(used, (key >> 14) & 7, 0)
    kind = jnp.where(used, (key >> 13) & 1, 0)
    place = jnp.minimum(key & 8191, limit)
    order = group * GROUP + lane
    degree = order + block * STEP + step
    number = 19 * group - (((group - 1) * (group - 1)) >> 2) + block
    ring = number & (RING - 1)
    number = jnp.where(used, number, LATE)
    at_value = (ring * SLOT + 1 + step) * WIDE + lane
    at_scale = ring * WIDE + lane
    target = place * PITCH
    m = order.astype(F32)
    first = degree - step
    product = jnp.ones_like(m)
    for q in range(STEP):
        j = first + q
        jf = j.astype(F32)
        ratio = (jf * jf - m * m) / (jf * jf - 0.25)
        product = jnp.where((j > order) & (j <= degree), product * ratio, product)
    return number, at_value, at_scale, degree, order * 2 + kind, target, lax.rsqrt(product)


def gather_kernel(theta_ref, lon_ref, ratio_ref, comp_ref, weight_ref, seen_ref, key_ref, *rest):
    outs = rest[:7]
    params_ref, local, everyone, send_sem, recv_sem = rest[7:]
    me = lax.axis_index("row")
    count = everyone.shape[0]
    half = theta_ref.shape[0]
    barrier = pltpu.get_barrier_semaphore()
    for d in range(1, count):
        pl.semaphore_signal(
            barrier, inc=1, device_id={"row": lax.rem(me + d, count)}, device_id_type=pl.DeviceIdType.MESH
        )
    local[...] = jnp.zeros_like(local)
    for k, ref in enumerate((theta_ref, lon_ref, ratio_ref, comp_ref, weight_ref, seen_ref)):
        local[pl.ds(k, 1), pl.ds(0, half)] = ref[...].astype(F32).reshape(1, half)
    pl.semaphore_wait(barrier, count - 1)

    def send(d):
        return pltpu.make_async_remote_copy(
            src_ref=local, dst_ref=everyone.at[me], send_sem=send_sem.at[d], recv_sem=recv_sem.at[d],
            device_id={"row": lax.rem(me + d, count)}, device_id_type=pl.DeviceIdType.MESH,
        )

    def receive(d):
        return pltpu.make_async_remote_copy(
            src_ref=local, dst_ref=everyone.at[lax.rem(me + count - d, count)],
            send_sem=send_sem.at[d], recv_sem=recv_sem.at[d],
            device_id={"row": lax.rem(me + d, count)}, device_id_type=pl.DeviceIdType.MESH,
        )

    for d in range(1, count):
        send(d).start()
    everyone[me] = local[...]
    for ref, value in zip(outs, list_facts(key_ref[...], LIMIT)):
        ref[...] = value
    for d in range(1, count):
        receive(d).wait_recv()
    left = lax.broadcasted_iota(I32, (8, 128), 1) < half
    for c in range(PARTS):
        merged = jnp.where(left, everyone[2 * c], pltpu.roll(everyone[2 * c + 1], half, 1))
        params_ref[pl.ds(c, 8, stride=8), :] = merged
    for d in range(1, count):
        send(d).wait_send()


LIMIT = 6656


def kernel(
    col_ref, number_hbm, value_hbm, scale_hbm, radial_hbm, harm_hbm, target_hbm, grow_hbm,
    params_ref, table_hbm, inv_ref, logs_ref, right_ref, normal_ref,
    out_ref, right_out_ref,
    number_ref, value_ref, scale_ref, radial_ref, harm_ref, target_ref, grow_ref,
    value_buf, scale_buf, harm_buf, radial_buf, design_buf, seed_buf, level_buf, table_ref,
    slab_hi, slab_lo, in_buf, out_buf, list_sem, in_sem, out_sem,
):
    rows, width = normal_ref.shape
    chunks = rows // CHUNK

    lists = [
        pltpu.make_async_copy(src, dst, list_sem.at[k])
        for k, (src, dst) in enumerate(
            (
                (table_hbm, table_ref),
                (number_hbm, number_ref),
                (value_hbm, value_ref),
                (scale_hbm, scale_ref),
                (radial_hbm, radial_ref),
                (harm_hbm, harm_ref),
                (target_hbm, target_ref),
                (grow_hbm, grow_ref),
            )
        )
    ]
    for copy in lists:
        copy.start()

    def fetch(index, slot):
        return pltpu.make_async_copy(
            normal_ref.at[pl.ds(pl.multiple_of(index * CHUNK, CHUNK), CHUNK)], in_buf.at[slot], in_sem.at[slot]
        )

    def put(index, slot):
        return pltpu.make_async_copy(
            out_buf.at[slot], out_ref.at[pl.ds(pl.multiple_of(index * CHUNK, CHUNK), CHUNK)], out_sem.at[slot]
        )

    for k in range(BUFS):
        fetch(k, k).start()

    def param(k):
        return params_ref[pl.ds(8 * k, 8), :]

    theta = param(0)
    lon = param(1)
    cos_t = jnp.cos(theta)
    sin_t = jnp.sin(theta)
    log_s = jnp.log(sin_t)
    comp = param(3)
    weight = param(4)
    scaled = weight * param(5)
    part0 = jnp.where(comp == 2.0, 1.0, jnp.where(comp == 1.0, 0.0, -1.0))
    part1 = jnp.where(comp == 2.0, 0.0, jnp.where(comp == 1.0, 1.0, -1.0))
    part1q = part1 / (sin_t * sin_t)
    inv_r = 1.0 / param(2)

    def spread(values, c):
        return jnp.broadcast_to(values[c : c + 1, :], (8, 128))

    twice = [spread(2.0 * cos_t, c) for c in range(PARTS)]
    logs = [spread(log_s, c) for c in range(PARTS)]
    subf = lax.broadcasted_iota(I32, (8, 128), 0).astype(F32)

    c1 = jnp.cos(lon)
    s1 = jnp.sin(lon)
    cs = [jnp.ones_like(c1)]
    sn = [jnp.zeros_like(c1)]
    for _ in range(8):
        cs.append(cs[-1] * c1 - sn[-1] * s1)
        sn.append(sn[-1] * c1 + cs[-2] * s1)
    c8, s8 = cs[8], sn[8]
    powers = [inv_r * inv_r * inv_r]
    step_r = inv_r
    for _ in range(7):
        powers.append(powers[-1] * inv_r)
    for _ in range(3):
        step_r = step_r * step_r

    def fill(block, carry):
        cc, ss, pw = carry
        base = block * 8
        for j in range(8):
            nf = (base + j).astype(F32)
            square = nf * nf
            harm_buf[(base + j) * 4] = cc[j]
            harm_buf[(base + j) * 4 + 1] = cc[j] * square
            harm_buf[(base + j) * 4 + 2] = ss[j]
            harm_buf[(base + j) * 4 + 3] = ss[j] * square
            inv_d = 1.0 / ((nf + 1.0) * (nf + 2.0))
            g = pw[j] * part1q * inv_d
            u = (cos_t * g) * (2.0 / (2.0 * nf - 1.0))
            radial_buf[(base + j) * 4] = pw[j] * (part0 - part1 * ((2.0 * nf + 1.0) * inv_d)) + nf * g
            radial_buf[(base + j) * 4 + 1] = g
            radial_buf[(base + j) * 4 + 2] = u * square
            radial_buf[(base + j) * 4 + 3] = u
        orders = subf + base.astype(F32)
        diag = logs_ref[pl.ds(pl.multiple_of(base, 8), 8), :]
        before = -1.0 / (1.0 - (orders * orders - 0.25) * inv_ref[pl.ds(pl.multiple_of(base, 8), 8), :])
        for c in range(PARTS):
            log_seed = diag + orders * logs[c]
            level = jnp.minimum(jnp.ceil(log_seed * (1.0 / LOG_BIG)), 0.0)
            at = pl.multiple_of(block * 64, 64) + c * 8
            seed_buf[pl.ds(at, 8), :] = jnp.exp(log_seed - level * LOG_BIG) * before
            level_buf[pl.ds(at, 8), :] = level * 64.0
        return (
            tuple(cc[j] * c8 - ss[j] * s8 for j in range(8)),
            tuple(ss[j] * c8 + cc[j] * s8 for j in range(8)),
            tuple(pw[j] * step_r for j in range(8)),
        )

    lax.fori_loop(0, GROUPS, fill, (tuple(cs[:8]), tuple(sn[:8]), tuple(powers)))

    for copy in lists:
        copy.wait()

    def make_row(j):
        at = value_ref[j]
        now = value_buf[pl.ds(at, 8, stride=PITCH), :]
        past = value_buf[pl.ds(at - WIDE, 8, stride=PITCH), :]
        scale = scale_buf[pl.ds(scale_ref[j], 8, stride=PITCH), :]
        n = radial_ref[j] * 4
        h = harm_ref[j] * 2
        body = harm_buf[h] * (now * radial_buf[n] - past * radial_buf[n + 2]) - harm_buf[h + 1] * (
            now * radial_buf[n + 1] - past * radial_buf[n + 3]
        )
        design_buf[pl.ds(target_ref[j], 8), :] = body * (scale * grow_ref[j])

    def drain(cursor, number):
        def more(at):
            return number_ref[at] <= number

        def piece(at):
            for u in range(DRAIN):
                make_row(at + u)
            kept = at + 0
            for u in range(DRAIN):
                kept = kept + (number_ref[at + u] <= number).astype(I32)
            return kept

        return lax.while_loop(more, piece, cursor)

    def group_body(group, carry):
        cursor, number = carry
        zero = jnp.zeros((8, 128), F32)
        orders = subf + (group * GROUP).astype(F32)
        squares = orders * orders - 0.25
        at = pl.multiple_of(group * 64, 64)
        one = tuple(zero for _ in range(PARTS))
        two = tuple(seed_buf[pl.ds(at + c * 8, 8), :] for c in range(PARTS))
        levels = tuple(level_buf[pl.ds(at + c * 8, 8), :] for c in range(PARTS))

        def factors(number):
            sigma = table_ref[pl.ds(pl.multiple_of(number * 8, 8), 8), :]
            return sigma, sigma * SMALL, 64.0 / sigma

        def block_body(block, carry):
            one, two, levels, (sigma, sigma_small, limit), cursor, number = carry
            one, two, levels = list(one), list(two), list(levels)
            cursor = drain(cursor, number - RING)
            ring = number & (RING - 1)
            first = pl.multiple_of(group * GROUP + block * STEP, 8)
            at_scale = ring * WIDE
            at_value = ring * (SLOT * WIDE)
            for c in range(PARTS):
                big = jnp.abs(one[c]) > limit
                factor = jnp.where(big, sigma_small, sigma)
                one[c] = one[c] * factor
                two[c] = two[c] * factor
                levels[c] = levels[c] + jnp.where(big, 64.0, 0.0)
                scale_buf[pl.ds(at_scale + c * PITCH, 8), :] = jnp.exp2(levels[c])
                value_buf[pl.ds(at_value + c * PITCH, 8), :] = one[c]
            for i in range(STEP):
                make_row(cursor + i)
                rho = 1.0 - squares * inv_ref[pl.ds(first + i, 8), :]
                fresh = [twice[c] * one[c] - rho * two[c] for c in range(PARTS)]
                for c in range(PARTS):
                    value_buf[pl.ds(at_value + (1 + i) * WIDE + c * PITCH, 8), :] = fresh[c]
                one, two = fresh, one
            done = jnp.int32(0)
            for half in (8, 4, 2, 1):
                done = done + jnp.where(number_ref[cursor + done + (half - 1)] < number, half, 0)
            done = done + (number_ref[cursor + done] < number).astype(I32)
            cursor = cursor + jnp.minimum(done, STEP)
            return tuple(one), tuple(two), tuple(levels), factors(number + 1), cursor, number + 1

        blocks = (NMAX + STEP - group * GROUP) // STEP
        out = lax.fori_loop(0, blocks, block_body, (one, two, levels, factors(number), cursor, number))
        return out[4], out[5]

    cursor, _ = lax.fori_loop(0, GROUPS, group_body, (jnp.int32(0), jnp.int32(0)))
    cursor = drain(cursor, BLOCKS)

    def clear(j, _):
        design_buf[pl.ds(target_ref[j], 8), :] = jnp.zeros((8, 128), F32)
        return 0

    lax.fori_loop(cursor, rows + width, clear, 0)

    def entries(first, count, c):
        return design_buf[pl.ds(first * PITCH + c, count, stride=PITCH), :]

    for c in range(PARTS):
        for half in range(width // 256):
            block = entries(rows + half * 256, 256, c)
            block = (block * weight[c : c + 1, :]).T
            hi = block.astype(BF16)
            slab_hi[pl.ds(c * 128, 128), pl.ds(half * 256, 256)] = hi
            slab_lo[pl.ds(c * 128, 128), pl.ds(half * 256, 256)] = (block - hi.astype(F32)).astype(BF16)

    own = right_ref.shape[0]
    total = jnp.zeros((own, 128), F32)
    at = col_ref[0] * own
    for c in range(PARTS):
        total = total + entries(at, own, c) * scaled[c : c + 1, :]
    summed = lax.dot_general(
        jnp.ones((8, 128), F32), total, (((1,), (1,)), ((), ())),
        precision=lax.Precision.HIGHEST, preferred_element_type=F32,
    )
    right_out_ref[...] = right_ref[...] + summed[0:1, :].reshape(own)

    def chunk_body(index, _):
        slot = lax.rem(index, BUFS)
        his = []
        los = []
        for c in range(PARTS):
            x = entries(index * CHUNK, CHUNK, c)
            hi = x.astype(BF16)
            his.append(hi)
            los.append((x - hi.astype(F32)).astype(BF16))
        hi = jnp.concatenate(his, axis=1)
        lo = jnp.concatenate(los, axis=1)
        update = jnp.dot(hi, slab_hi[...], preferred_element_type=F32)
        update += jnp.dot(hi, slab_lo[...], preferred_element_type=F32)
        update += jnp.dot(lo, slab_hi[...], preferred_element_type=F32)
        fetch(index, slot).wait()

        @pl.when(index >= BUFS)
        def _():
            put(index - BUFS, slot).wait()

        out_buf[slot] = in_buf[slot] + update
        put(index, slot).start()

        @pl.when(index + BUFS < chunks)
        def _():
            fetch(index + BUFS, slot).start()

        return 0

    lax.fori_loop(0, chunks, chunk_body, 0)
    for k in range(BUFS):
        put(chunks - BUFS + k, k).wait()


def local_update(params, col, facts, normal_slab, right_side):
    rows, width = normal_slab.shape
    own = right_side.shape[0]
    entries = facts[0].shape[0]
    smem = pl.BlockSpec(memory_space=pltpu.SMEM)
    vmem = pl.BlockSpec(memory_space=pltpu.VMEM)
    hbm = pl.BlockSpec(memory_space=pltpu.HBM)
    return pl.pallas_call(
        kernel,
        out_shape=(
            jax.ShapeDtypeStruct((rows, width), F32),
            jax.ShapeDtypeStruct((own,), F32),
        ),
        in_specs=[smem] + [hbm] * 7 + [vmem, hbm, vmem, vmem, vmem, hbm],
        out_specs=(hbm, vmem),
        scratch_shapes=[pltpu.SMEM((entries,), I32)] * 6
        + [pltpu.SMEM((entries,), F32)]
        + [
            pltpu.VMEM((RING * SLOT * WIDE, 128), F32),
            pltpu.VMEM((RING * WIDE, 128), F32),
            pltpu.VMEM((TOP * 4, 8, 128), F32),
            pltpu.VMEM((TOP * 4, 8, 128), F32),
            pltpu.VMEM(((rows + width + 1) * PITCH, 128), F32),
            pltpu.VMEM((GROUPS * 64, 128), F32),
            pltpu.VMEM((GROUPS * 64, 128), F32),
            pltpu.VMEM((BLOCKS * 8 + 8, 128), F32),
            pltpu.VMEM((OBS, width), BF16),
            pltpu.VMEM((OBS, width), BF16),
            pltpu.VMEM((BUFS, CHUNK, width), F32),
            pltpu.VMEM((BUFS, CHUNK, width), F32),
            pltpu.SemaphoreType.DMA((8,)),
            pltpu.SemaphoreType.DMA((BUFS,)),
            pltpu.SemaphoreType.DMA((BUFS,)),
        ],
        compiler_params=pltpu.CompilerParams(vmem_limit_bytes=62 * 1024 * 1024),
        name="normal_update",
    )(
        col, *facts, params, jnp.asarray(block_scales()), jnp.asarray(inverse_squares()),
        jnp.asarray(diagonal_logs()), right_side, normal_slab,
    )


def on_device(
    colatitude, longitude, radius_ratio, component, obs_weight, observed,
    unknown_map, slab_map, normal_slab, right_side,
):
    rows, width = normal_slab.shape
    unknowns = lax.dynamic_slice_in_dim(unknown_map, lax.axis_index("row") * rows, rows, axis=1)
    col = lax.axis_index("col").astype(I32).reshape(1)
    key = lax.sort(list_keys(unknowns, slab_map), is_stable=False)
    entries = key.shape[0]
    shape = (entries // 128, 128)
    count = lax.axis_size("row")
    vmem = pl.BlockSpec(memory_space=pltpu.VMEM)
    outs = pl.pallas_call(
        gather_kernel,
        out_shape=tuple(jax.ShapeDtypeStruct(shape, I32) for _ in range(6))
        + (jax.ShapeDtypeStruct(shape, F32), jax.ShapeDtypeStruct((64, 128), F32)),
        in_specs=[vmem] * 7,
        out_specs=(vmem,) * 8,
        scratch_shapes=[
            pltpu.VMEM((8, 128), F32),
            pltpu.VMEM((count, 8, 128), F32),
            pltpu.SemaphoreType.DMA((count,)),
            pltpu.SemaphoreType.DMA((count,)),
        ],
        compiler_params=pltpu.CompilerParams(collective_id=0, has_side_effects=True),
        name="gather_observations",
    )(colatitude, longitude, radius_ratio, component, obs_weight, observed, key.reshape(shape))
    facts = tuple(x.reshape(entries) for x in outs[:7])
    return local_update(outs[7], col, facts, normal_slab, right_side)


def solution(mesh):
    return jax.shard_map(
        on_device,
        mesh=mesh,
        in_specs=(
            P("row"), P("row"), P("row"), P("row"), P("row"), P("row"),
            P(), P(None, "col"), P("row", "col"), P(("row", "col")),
        ),
        out_specs=(P("row", "col"), P(("row", "col"))),
        check_vma=False,
    )
```

time: 187 us -> 106 us (0.57)
  blocking collectives: 27.2 us -> 0 us
  local copies, waits for them, and re-layouts: 27.9 us -> 2.06 us
  Pallas kernels: 120 us -> 96.5 us
  other arithmetic: 11.4 us -> 6.23 us
    pallas_call x1, Pallas kernels: 120 us -> 83.5 us  [local_update(): pl.pallas_call(kernel, out_shape=(jax.ShapeDtypeStruct((rows, width), F32...]
    all_gather x1 -> x0, blocking collectives: 27.2 us -> none  [on_device(): params = lax.all_gather(local, 'row', axis=0)]
    concatenate x14 -> x0, local copies, waits for them, and re-layouts: 17.1 us -> none  [local_update(): jnp.concatenate([x, x[:1] + jnp.zeros((pad,), x.dtype)])]
    pallas_call x0 -> x1, Pallas kernels: none -> 13 us  [on_device(): pl.pallas_call(gather_kernel, out_shape=tuple((jax.ShapeDtypeStruct(shape...]
    slice x15 -> x2, local copies, waits for them, and re-layouts: 8.16 us -> 2.06 us  [the longest x1 1.24 us: list_keys(): unknowns[2]]
    reshape x2 -> x0, local copies, waits for them, and re-layouts: 1.94 us -> none  [the longest x1 1.27 us: local_update(): right_side.reshape(1, own)]
where the time goes in v2:
time: 106 us; the launch traced here: 105 us
  Pallas kernels  96.5 us (91%)
  other arithmetic  6.23 us (6%)
  local copies, waits for them, and re-layouts  2.06 us (2%)
    pallas_call x1, Pallas kernels, local_update(): pl.pallas_call(kernel, out_shape=(jax.ShapeDtypeStruct((rows, width), F32...  83.5 us
    pallas_call x1, Pallas kernels, on_device(): pl.pallas_call(gather_kernel, out_shape=tuple((jax.ShapeDtypeStruct(shape...  13 us
    sort x1, other arithmetic, on_device(): key = lax.sort(list_keys(unknowns, slab_map), is_stable=False)  6.19 us

profile of v2, /device:TPU:1, one launch (start us, length us, event | category | flops | bytes accessed | tf_op | source)
XLA Modules:
  0.0 105.5 jit_solution(16465405295168045861)
XLA Ops:
  0.6 0.8 fusion.2
  1.5 1.2 %fusion.1 = (s32[1,6144]{1,0:T(1,128)S(1)}, s32[1,6144]{1,0:T(1,128)S(1)}, s32[1,6144]{1,0:T(1,128)S(1)}) fusion(s32[3,98304]{1,0:T(4,128)} %param.19, s32[]{:T(128)S(6)} %add.11, s32[]{:T(128)S(6)} %select_n.7, s32[]{:T(128)S(6)} %add.12), kind=kLoop, calls=%fused_computation.6 | loop fusion | bytes 147468 | tf_op jit(solution)/shard_map/slice | solution.py:74
  2.7 6.2 %sort.7 = s32[7168]{0:T(1024)} sort(s32[7168]{0:T(1024)S(1)} %or_select_fusion), dimensions={0}, to_apply=%region_0.1 | sort | flops 93184 | bytes 57344 | tf_op jit(solution)/shard_map/sort | solution.py:468
  8.9 13.0 %gather_observations.1 = (s32[56,128]{1,0:T(8,128)}, s32[56,128]{1,0:T(8,128)}, s32[56,128]{1,0:T(8,128)}, s32[56,128]{1,0:T(8,128)}, s32[56,128]{1,0:T(8,128)},...) custom-call(f32[64]{0:T(128)} %theta_ref.1, f32[64]{0:T(128)} %lon_ref.1, f32[64]{0:T(128)} %ratio_ref.1, ...), custom_call_target="tpu_custom_call" | custom-call | tf_op jit(solution)/shard_map/gather_observations/pallas_call | solution.py:473
  22.0 83.5 %normal_update.1 = (f32[6144,512]{1,0:T(8,128)}, f32[768]{0:T(1024)}) custom-call(s32[1]{0:T(128)} %bitcast.col_ref, s32[7168]{0:T(1024)} %bitcast.19, s32[7168]{0:T(1024)} %bitcast.20, s32[7168]{0:T(1024)} %bitcast.21, s32[7168]{0:T(1024)} %bitcast.22, s32[7168]{0:T(1024)} %bitcast.23, s32[7168]{0:T(1024)} %bitcast.24, f32[7168]{0:T(1024)} %bitcast.25, ...), custom_call_target="tpu_custom_call" | custom-call | tf_op jit(solution)/shard_map/normal_update/pallas_call | solution.py:426
  (3 shorter events, 0.0 us)

commit v3 on v2

--- a/solution.py
+++ b/solution.py
@@ -15,10 +15,11 @@
 PITCH = 9
 WIDE = 8 * PITCH
 RING = 8
-BUFS = 4
+BUFS = 2
 OBS = 1024
 PARTS = 8
-CHUNK = 256
+CHUNK = 512
+PACE = 16
 DRAIN = 8
 LATE = 1 << 20
 BIG = float(2.0**64)
@@ -65,14 +66,7 @@
 BLOCKS = sum(blocks_of(group) for group in range(GROUPS))
 
 
-def list_keys(unknowns, slab_map):
-    rows = unknowns.shape[1]
-    width = slab_map.shape[1]
-    total = -(-(rows + width + 64) // 1024) * 1024
-    degree = jnp.concatenate([unknowns[0], slab_map[0], jnp.full((total - rows - width,), 2, I32)])
-    order = jnp.concatenate([unknowns[1], slab_map[1], jnp.zeros((total - rows - width,), I32)])
-    kind = jnp.concatenate([unknowns[2], slab_map[2], jnp.full((total - rows - width,), 2, I32)])
-    place = lax.broadcasted_iota(I32, (total,), 0)
+def row_key(degree, order, kind, place):
     beyond = degree - order
     key = (
         (((order >> 3) - 32) << 26)
@@ -83,6 +77,29 @@
         | place
     )
     return jnp.where(kind == 2, (31 << 26) | place, key)
+
+
+def sort_keys(key):
+    height = key.shape[0]
+    total = height * 128
+    row = lax.broadcasted_iota(I32, key.shape, 0)
+    lane = lax.broadcasted_iota(I32, key.shape, 1)
+    index = row * 128 + lane
+    size = 2
+    while size <= total:
+        rising = (index & size) == 0
+        stride = size // 2
+        while stride >= 1:
+            low = (index & stride) == 0
+            if stride < 128:
+                ahead, behind = pltpu.roll(key, 128 - stride, 1), pltpu.roll(key, stride, 1)
+            else:
+                ahead, behind = pltpu.roll(key, height - stride // 128, 0), pltpu.roll(key, stride // 128, 0)
+            other = jnp.where(low, ahead, behind)
+            key = jnp.where(low == rising, jnp.minimum(key, other), jnp.maximum(key, other))
+            stride //= 2
+        size *= 2
+    return key
 
 
 def list_facts(key, limit):
@@ -110,15 +127,25 @@
         jf = j.astype(F32)
         ratio = (jf * jf - m * m) / (jf * jf - 0.25)
         product = jnp.where((j > order) & (j <= degree), product * ratio, product)
-    return number, at_value, at_scale, degree, order * 2 + kind, target, lax.rsqrt(product)
-
-
-def gather_kernel(theta_ref, lon_ref, ratio_ref, comp_ref, weight_ref, seen_ref, key_ref, *rest):
-    outs = rest[:7]
-    params_ref, local, everyone, send_sem, recv_sem = rest[7:]
+    places = (at_value << 16) | target
+    factors = (degree << 18) | ((order * 2 + kind) * 2)
+    return number, at_scale, places, factors, lax.rsqrt(product)
+
+
+def gather_kernel(
+    theta_ref, lon_ref, ratio_ref, comp_ref, weight_ref, seen_ref, unknown_ref, slab_ref,
+    number_ref, scale_ref, places_ref, factors_ref, grow_ref, params_ref,
+    local, everyone, map_buf, key_buf, send_sem, recv_sem, map_sem,
+):
     me = lax.axis_index("row")
     count = everyone.shape[0]
     half = theta_ref.shape[0]
+    rows = map_buf.shape[1]
+    width = slab_ref.shape[1]
+    read_map = pltpu.make_async_copy(
+        unknown_ref.at[:, pl.ds(pl.multiple_of(me * rows, 128), rows)], map_buf, map_sem.at[0]
+    )
+    read_map.start()
     barrier = pltpu.get_barrier_semaphore()
     for d in range(1, count):
         pl.semaphore_signal(
@@ -145,7 +172,16 @@
     for d in range(1, count):
         send(d).start()
     everyone[me] = local[...]
-    for ref, value in zip(outs, list_facts(key_ref[...], LIMIT)):
+    read_map.wait()
+    lanes = lax.broadcasted_iota(I32, (1, 128), 1)
+    for t in range((rows + width) // 128):
+        ref, at = (map_buf, t * 128) if t * 128 < rows else (slab_ref, t * 128 - rows)
+        part = [ref[pl.ds(k, 1), pl.ds(at, 128)] for k in range(3)]
+        key_buf[pl.ds(t, 1), :] = row_key(part[0], part[1], part[2], lanes + t * 128)
+    place = lax.broadcasted_iota(I32, key_buf.shape, 0) * 128 + lax.broadcasted_iota(I32, key_buf.shape, 1)
+    key = sort_keys(jnp.where(place < rows + width, key_buf[...], (31 << 26) | place))
+    facts = list_facts(key[: number_ref.shape[0]], rows + width)
+    for ref, value in zip((number_ref, scale_ref, places_ref, factors_ref, grow_ref), facts):
         ref[...] = value
     for d in range(1, count):
         receive(d).wait_recv()
@@ -157,14 +193,11 @@
         send(d).wait_send()
 
 
-LIMIT = 6656
-
-
 def kernel(
-    col_ref, number_hbm, value_hbm, scale_hbm, radial_hbm, harm_hbm, target_hbm, grow_hbm,
+    col_ref, number_hbm, scale_hbm, places_hbm, factors_hbm, grow_hbm,
     params_ref, table_hbm, inv_ref, logs_ref, right_ref, normal_ref,
     out_ref, right_out_ref,
-    number_ref, value_ref, scale_ref, radial_ref, harm_ref, target_ref, grow_ref,
+    number_ref, scale_ref, places_ref, factors_ref, grow_ref,
     value_buf, scale_buf, harm_buf, radial_buf, design_buf, seed_buf, level_buf, table_ref,
     slab_hi, slab_lo, in_buf, out_buf, list_sem, in_sem, out_sem,
 ):
@@ -177,11 +210,9 @@
             (
                 (table_hbm, table_ref),
                 (number_hbm, number_ref),
-                (value_hbm, value_ref),
                 (scale_hbm, scale_ref),
-                (radial_hbm, radial_ref),
-                (harm_hbm, harm_ref),
-                (target_hbm, target_ref),
+                (places_hbm, places_ref),
+                (factors_hbm, factors_ref),
                 (grow_hbm, grow_ref),
             )
         )
@@ -278,16 +309,18 @@
         copy.wait()
 
     def make_row(j):
-        at = value_ref[j]
+        places = places_ref[j]
+        factors = factors_ref[j]
+        at = places >> 16
         now = value_buf[pl.ds(at, 8, stride=PITCH), :]
         past = value_buf[pl.ds(at - WIDE, 8, stride=PITCH), :]
         scale = scale_buf[pl.ds(scale_ref[j], 8, stride=PITCH), :]
-        n = radial_ref[j] * 4
-        h = harm_ref[j] * 2
+        n = factors >> 16
+        h = factors & 65535
         body = harm_buf[h] * (now * radial_buf[n] - past * radial_buf[n + 2]) - harm_buf[h + 1] * (
             now * radial_buf[n + 1] - past * radial_buf[n + 3]
         )
-        design_buf[pl.ds(target_ref[j], 8), :] = body * (scale * grow_ref[j])
+        design_buf[pl.ds(places & 65535, 8), :] = body * (scale * grow_ref[j])
 
     def drain(cursor, number):
         def more(at):
@@ -334,17 +367,17 @@
                 scale_buf[pl.ds(at_scale + c * PITCH, 8), :] = jnp.exp2(levels[c])
                 value_buf[pl.ds(at_value + c * PITCH, 8), :] = one[c]
             for i in range(STEP):
-                make_row(cursor + i)
+                for k in range(i * PACE // STEP, (i + 1) * PACE // STEP):
+                    make_row(cursor + k)
                 rho = 1.0 - squares * inv_ref[pl.ds(first + i, 8), :]
                 fresh = [twice[c] * one[c] - rho * two[c] for c in range(PARTS)]
                 for c in range(PARTS):
                     value_buf[pl.ds(at_value + (1 + i) * WIDE + c * PITCH, 8), :] = fresh[c]
                 one, two = fresh, one
             done = jnp.int32(0)
-            for half in (8, 4, 2, 1):
+            for half in (8, 4, 2, 1, 1):
                 done = done + jnp.where(number_ref[cursor + done + (half - 1)] < number, half, 0)
-            done = done + (number_ref[cursor + done] < number).astype(I32)
-            cursor = cursor + jnp.minimum(done, STEP)
+            cursor = cursor + jnp.minimum(done, PACE)
             return tuple(one), tuple(two), tuple(levels), factors(number + 1), cursor, number + 1
 
         blocks = (NMAX + STEP - group * GROUP) // STEP
@@ -355,7 +388,7 @@
     cursor = drain(cursor, BLOCKS)
 
     def clear(j, _):
-        design_buf[pl.ds(target_ref[j], 8), :] = jnp.zeros((8, 128), F32)
+        design_buf[pl.ds(places_ref[j] & 65535, 8), :] = jnp.zeros((8, 128), F32)
         return 0
 
     lax.fori_loop(cursor, rows + width, clear, 0)
@@ -429,9 +462,9 @@
             jax.ShapeDtypeStruct((rows, width), F32),
             jax.ShapeDtypeStruct((own,), F32),
         ),
-        in_specs=[smem] + [hbm] * 7 + [vmem, hbm, vmem, vmem, vmem, hbm],
+        in_specs=[smem] + [hbm] * 5 + [vmem, hbm, vmem, vmem, vmem, hbm],
         out_specs=(hbm, vmem),
-        scratch_shapes=[pltpu.SMEM((entries,), I32)] * 6
+        scratch_shapes=[pltpu.SMEM((entries,), I32)] * 4
         + [pltpu.SMEM((entries,), F32)]
         + [
             pltpu.VMEM((RING * SLOT * WIDE, 128), F32),
@@ -446,7 +479,7 @@
             pltpu.VMEM((OBS, width), BF16),
             pltpu.VMEM((BUFS, CHUNK, width), F32),
             pltpu.VMEM((BUFS, CHUNK, width), F32),
-            pltpu.SemaphoreType.DMA((8,)),
+            pltpu.SemaphoreType.DMA((6,)),
             pltpu.SemaphoreType.DMA((BUFS,)),
             pltpu.SemaphoreType.DMA((BUFS,)),
         ],
@@ -463,30 +496,32 @@
     unknown_map, slab_map, normal_slab, right_side,
 ):
     rows, width = normal_slab.shape
-    unknowns = lax.dynamic_slice_in_dim(unknown_map, lax.axis_index("row") * rows, rows, axis=1)
     col = lax.axis_index("col").astype(I32).reshape(1)
-    key = lax.sort(list_keys(unknowns, slab_map), is_stable=False)
-    entries = key.shape[0]
+    entries = -(-(rows + width + 2 * PACE) // 1024) * 1024
+    total = 1 << (rows + width - 1).bit_length()
     shape = (entries // 128, 128)
     count = lax.axis_size("row")
     vmem = pl.BlockSpec(memory_space=pltpu.VMEM)
     outs = pl.pallas_call(
         gather_kernel,
-        out_shape=tuple(jax.ShapeDtypeStruct(shape, I32) for _ in range(6))
+        out_shape=tuple(jax.ShapeDtypeStruct(shape, I32) for _ in range(4))
         + (jax.ShapeDtypeStruct(shape, F32), jax.ShapeDtypeStruct((64, 128), F32)),
-        in_specs=[vmem] * 7,
-        out_specs=(vmem,) * 8,
+        in_specs=[vmem] * 6 + [pl.BlockSpec(memory_space=pltpu.HBM), vmem],
+        out_specs=(vmem,) * 6,
         scratch_shapes=[
             pltpu.VMEM((8, 128), F32),
             pltpu.VMEM((count, 8, 128), F32),
+            pltpu.VMEM((3, rows), I32),
+            pltpu.VMEM((total // 128, 128), I32),
             pltpu.SemaphoreType.DMA((count,)),
             pltpu.SemaphoreType.DMA((count,)),
+            pltpu.SemaphoreType.DMA((1,)),
         ],
         compiler_params=pltpu.CompilerParams(collective_id=0, has_side_effects=True),
         name="gather_observations",
-    )(colatitude, longitude, radius_ratio, component, obs_weight, observed, key.reshape(shape))
-    facts = tuple(x.reshape(entries) for x in outs[:7])
-    return local_update(outs[7], col, facts, normal_slab, right_side)
+    )(colatitude, longitude, radius_ratio, component, obs_weight, observed, unknown_map, slab_map)
+    facts = tuple(x.reshape(entries) for x in outs[:5])
+    return local_update(outs[5], col, facts, normal_slab, right_side)
 
 
 def solution(mesh):

time: 106 us -> 99.7 us (0.941)
  other arithmetic: 6.23 us -> 0 us
  Pallas kernels: 96.5 us -> 98.8 us
  local copies, waits for them, and re-layouts: 2.06 us -> 0 us
    sort x1 -> x0, other arithmetic: 6.19 us -> none  [on_device(): key = lax.sort(list_keys(unknowns, slab_map), is_stable=False)]
    pallas_call x1, Pallas kernels: 13 us -> 16 us  [on_device(): pl.pallas_call(gather_kernel, out_shape=tuple((jax.ShapeDtypeStruct(shape...]
    slice x2 -> x0, local copies, waits for them, and re-layouts: 2.06 us -> none  [the longest x1 1.24 us: list_keys(): unknowns[2]]
where the time goes in v3:
time: 99.7 us; the launch traced here: 99.5 us
  Pallas kernels  98.8 us (99%)
    pallas_call x1, Pallas kernels, local_update(): pl.pallas_call(kernel, out_shape=(jax.ShapeDtypeStruct((rows, width), F32...  82.9 us
    pallas_call x1, Pallas kernels, on_device(): pl.pallas_call(gather_kernel, out_shape=tuple((jax.ShapeDtypeStruct(shape...  16 us

profile of v3, /device:TPU:1, one launch (start us, length us, event | category | flops | bytes accessed | tf_op | source)
XLA Modules:
  0.0 99.5 jit_solution(5497837006532988141)
XLA Ops:
  0.6 16.0 %gather_observations.1 = (s32[56,128]{1,0:T(8,128)}, s32[56,128]{1,0:T(8,128)}, s32[56,128]{1,0:T(8,128)}, s32[56,128]{1,0:T(8,128)}, f32[56,128]{1,0:T(8,128)}, /*index=5*/f32[64,128]{1,0:T(8,128)}) custom-call(f32[64]{0:T(128)} %theta_ref.1, f32[64]{0:T(128)} %lon_ref.1, f32[64]{0:T(128)} %ratio_ref.1, s32[64]{0:T(128)} %comp_ref.1, f32[64]{0:T(128)} %weight_ref.1, ...), custom_call_target="tpu_custom_call" | custom-call | tf_op jit(solution)/shard_map/gather_observations/pallas_call | solution.py:505
  16.6 82.9 %normal_update.1 = (f32[6144,512]{1,0:T(8,128)}, f32[768]{0:T(1024)}) custom-call(s32[1]{0:T(128)} %bitcast.col_ref, s32[7168]{0:T(1024)} %bitcast.6, s32[7168]{0:T(1024)} %bitcast.7, s32[7168]{0:T(1024)} %bitcast.8, s32[7168]{0:T(1024)} %bitcast.9, f32[7168]{0:T(1024)} %bitcast.10, f32[64,128]{1,0:T(8,128)} %get-tuple-element.13.params_ref, ...), custom_call_target="tpu_custom_call" | custom-call | tf_op jit(solution)/shard_map/normal_update/pallas_call | solution.py:459

commit v4 on v3

--- a/solution.py
+++ b/solution.py
@@ -18,15 +18,17 @@
 BUFS = 2
 OBS = 1024
 PARTS = 8
-CHUNK = 512
+CHUNK = 768
 PACE = 16
-DRAIN = 8
+BATCH = 2
+DRAIN = 16
 LATE = 1 << 20
 BIG = float(2.0**64)
 SMALL = float(2.0**-64)
 LOG_BIG = float(64.0 * np.log(2.0))
 F32 = jnp.float32
 BF16 = jnp.bfloat16
+F8 = jnp.float8_e4m3fn
 I32 = jnp.int32
 
 
@@ -127,14 +129,13 @@
         jf = j.astype(F32)
         ratio = (jf * jf - m * m) / (jf * jf - 0.25)
         product = jnp.where((j > order) & (j <= degree), product * ratio, product)
-    places = (at_value << 16) | target
-    factors = (degree << 18) | ((order * 2 + kind) * 2)
-    return number, at_scale, places, factors, lax.rsqrt(product)
+    at_harm = (order * 2 + kind) * 16
+    return number, at_value, at_scale, degree * 32, at_harm, target, lax.rsqrt(product)
 
 
 def gather_kernel(
     theta_ref, lon_ref, ratio_ref, comp_ref, weight_ref, seen_ref, unknown_ref, slab_ref,
-    number_ref, scale_ref, places_ref, factors_ref, grow_ref, params_ref,
+    number_ref, value_ref, scale_ref, radial_ref, harm_ref, target_ref, grow_ref, params_ref,
     local, everyone, map_buf, key_buf, send_sem, recv_sem, map_sem,
 ):
     me = lax.axis_index("row")
@@ -181,7 +182,8 @@
     place = lax.broadcasted_iota(I32, key_buf.shape, 0) * 128 + lax.broadcasted_iota(I32, key_buf.shape, 1)
     key = sort_keys(jnp.where(place < rows + width, key_buf[...], (31 << 26) | place))
     facts = list_facts(key[: number_ref.shape[0]], rows + width)
-    for ref, value in zip((number_ref, scale_ref, places_ref, factors_ref, grow_ref), facts):
+    outs = (number_ref, value_ref, scale_ref, radial_ref, harm_ref, target_ref, grow_ref)
+    for ref, value in zip(outs, facts):
         ref[...] = value
     for d in range(1, count):
         receive(d).wait_recv()
@@ -194,10 +196,10 @@
 
 
 def kernel(
-    col_ref, number_hbm, scale_hbm, places_hbm, factors_hbm, grow_hbm,
+    col_ref, number_hbm, value_hbm, scale_hbm, radial_hbm, harm_hbm, target_hbm, grow_hbm,
     params_ref, table_hbm, inv_ref, logs_ref, right_ref, normal_ref,
     out_ref, right_out_ref,
-    number_ref, scale_ref, places_ref, factors_ref, grow_ref,
+    number_ref, value_ref, scale_ref, radial_ref, harm_ref, target_ref, grow_ref,
     value_buf, scale_buf, harm_buf, radial_buf, design_buf, seed_buf, level_buf, table_ref,
     slab_hi, slab_lo, in_buf, out_buf, list_sem, in_sem, out_sem,
 ):
@@ -210,9 +212,11 @@
             (
                 (table_hbm, table_ref),
                 (number_hbm, number_ref),
+                (value_hbm, value_ref),
                 (scale_hbm, scale_ref),
-                (places_hbm, places_ref),
-                (factors_hbm, factors_ref),
+                (radial_hbm, radial_ref),
+                (harm_hbm, harm_ref),
+                (target_hbm, target_ref),
                 (grow_hbm, grow_ref),
             )
         )
@@ -277,17 +281,17 @@
         for j in range(8):
             nf = (base + j).astype(F32)
             square = nf * nf
-            harm_buf[(base + j) * 4] = cc[j]
-            harm_buf[(base + j) * 4 + 1] = cc[j] * square
-            harm_buf[(base + j) * 4 + 2] = ss[j]
-            harm_buf[(base + j) * 4 + 3] = ss[j] * square
+            harm_buf[pl.ds(pl.multiple_of(base * 32, 32) + j * 32, 8), :] = cc[j]
+            harm_buf[pl.ds(pl.multiple_of(base * 32, 32) + j * 32 + 8, 8), :] = cc[j] * square
+            harm_buf[pl.ds(pl.multiple_of(base * 32, 32) + j * 32 + 16, 8), :] = ss[j]
+            harm_buf[pl.ds(pl.multiple_of(base * 32, 32) + j * 32 + 24, 8), :] = ss[j] * square
             inv_d = 1.0 / ((nf + 1.0) * (nf + 2.0))
             g = pw[j] * part1q * inv_d
             u = (cos_t * g) * (2.0 / (2.0 * nf - 1.0))
-            radial_buf[(base + j) * 4] = pw[j] * (part0 - part1 * ((2.0 * nf + 1.0) * inv_d)) + nf * g
-            radial_buf[(base + j) * 4 + 1] = g
-            radial_buf[(base + j) * 4 + 2] = u * square
-            radial_buf[(base + j) * 4 + 3] = u
+            radial_buf[pl.ds(pl.multiple_of(base * 32, 32) + j * 32, 8), :] = pw[j] * (part0 - part1 * ((2.0 * nf + 1.0) * inv_d)) + nf * g
+            radial_buf[pl.ds(pl.multiple_of(base * 32, 32) + j * 32 + 8, 8), :] = g
+            radial_buf[pl.ds(pl.multiple_of(base * 32, 32) + j * 32 + 16, 8), :] = u * square
+            radial_buf[pl.ds(pl.multiple_of(base * 32, 32) + j * 32 + 24, 8), :] = u
         orders = subf + base.astype(F32)
         diag = logs_ref[pl.ds(pl.multiple_of(base, 8), 8), :]
         before = -1.0 / (1.0 - (orders * orders - 0.25) * inv_ref[pl.ds(pl.multiple_of(base, 8), 8), :])
@@ -309,18 +313,16 @@
         copy.wait()
 
     def make_row(j):
-        places = places_ref[j]
-        factors = factors_ref[j]
-        at = places >> 16
+        at = value_ref[j]
         now = value_buf[pl.ds(at, 8, stride=PITCH), :]
         past = value_buf[pl.ds(at - WIDE, 8, stride=PITCH), :]
         scale = scale_buf[pl.ds(scale_ref[j], 8, stride=PITCH), :]
-        n = factors >> 16
-        h = factors & 65535
-        body = harm_buf[h] * (now * radial_buf[n] - past * radial_buf[n + 2]) - harm_buf[h + 1] * (
-            now * radial_buf[n + 1] - past * radial_buf[n + 3]
-        )
-        design_buf[pl.ds(places & 65535, 8), :] = body * (scale * grow_ref[j])
+        n = pl.multiple_of(radial_ref[j], 32)
+        h = pl.multiple_of(harm_ref[j], 16)
+        kept = now * radial_buf[pl.ds(n, 8), :] - past * radial_buf[pl.ds(n + 16, 8), :]
+        spun = now * radial_buf[pl.ds(n + 8, 8), :] - past * radial_buf[pl.ds(n + 24, 8), :]
+        body = harm_buf[pl.ds(h, 8), :] * kept - harm_buf[pl.ds(h + 8, 8), :] * spun
+        design_buf[pl.ds(target_ref[j], 8), :] = body * (scale * grow_ref[j])
 
     def drain(cursor, number):
         def more(at):
@@ -364,16 +366,18 @@
                 one[c] = one[c] * factor
                 two[c] = two[c] * factor
                 levels[c] = levels[c] + jnp.where(big, 64.0, 0.0)
-                scale_buf[pl.ds(at_scale + c * PITCH, 8), :] = jnp.exp2(levels[c])
                 value_buf[pl.ds(at_value + c * PITCH, 8), :] = one[c]
             for i in range(STEP):
-                for k in range(i * PACE // STEP, (i + 1) * PACE // STEP):
-                    make_row(cursor + k)
+                if i % BATCH == 0:
+                    for k in range(i * PACE // STEP, (i + BATCH) * PACE // STEP):
+                        make_row(cursor + k)
                 rho = 1.0 - squares * inv_ref[pl.ds(first + i, 8), :]
                 fresh = [twice[c] * one[c] - rho * two[c] for c in range(PARTS)]
                 for c in range(PARTS):
                     value_buf[pl.ds(at_value + (1 + i) * WIDE + c * PITCH, 8), :] = fresh[c]
                 one, two = fresh, one
+            for c in range(PARTS):
+                scale_buf[pl.ds(at_scale + c * PITCH, 8), :] = jnp.exp2(levels[c])
             done = jnp.int32(0)
             for half in (8, 4, 2, 1, 1):
                 done = done + jnp.where(number_ref[cursor + done + (half - 1)] < number, half, 0)
@@ -387,22 +391,36 @@
     cursor, _ = lax.fori_loop(0, GROUPS, group_body, (jnp.int32(0), jnp.int32(0)))
     cursor = drain(cursor, BLOCKS)
 
-    def clear(j, _):
-        design_buf[pl.ds(places_ref[j] & 65535, 8), :] = jnp.zeros((8, 128), F32)
+    def clear(piece, _):
+        for u in range(DRAIN):
+            design_buf[pl.ds(target_ref[cursor + piece * DRAIN + u], 8), :] = zero
         return 0
 
-    lax.fori_loop(cursor, rows + width, clear, 0)
+    zero = jnp.zeros((8, 128), F32)
+    lax.fori_loop(0, (rows + width - cursor + DRAIN - 1) // DRAIN, clear, 0)
 
     def entries(first, count, c):
         return design_buf[pl.ds(first * PITCH + c, count, stride=PITCH), :]
 
+    peak = jnp.full((8, 128), 1e-30, F32)
+    for c in range(PARTS):
+        block = jnp.abs(entries(rows, width, c) * weight[c : c + 1, :])
+        peak = jnp.maximum(peak, jnp.max(block.reshape(width // 8, 8, 128), axis=0))
+    peak = jnp.max(peak, axis=(0, 1), keepdims=True)
+    shrink = jnp.exp2(jnp.ceil(jnp.log2(jnp.broadcast_to(peak, (8, 128)))) - 7.0)[0:1, :]
+    grow = 1.0 / shrink
     for c in range(PARTS):
         for half in range(width // 256):
             block = entries(rows + half * 256, 256, c)
             block = (block * weight[c : c + 1, :]).T
             hi = block.astype(BF16)
-            slab_hi[pl.ds(c * 128, 128), pl.ds(half * 256, 256)] = hi
-            slab_lo[pl.ds(c * 128, 128), pl.ds(half * 256, 256)] = (block - hi.astype(F32)).astype(BF16)
+            lo = block - hi.astype(F32)
+            cols = pl.ds(half * 256, 256)
+            factor = jnp.concatenate([grow, grow], axis=1)
+            slab_hi[pl.ds(c * 128, 128), cols] = hi
+            slab_lo[pl.ds(c * 128, 128), cols] = (block * factor).astype(F8)
+            slab_lo[pl.ds(OBS + c * 128, 128), cols] = (lo * (factor * 512.0)).astype(F8)
+    shrink = jnp.concatenate([shrink] * (width // 128), axis=1) * (1.0 / 512.0)
 
     own = right_ref.shape[0]
     total = jnp.zeros((own, 128), F32)
@@ -419,16 +437,15 @@
         slot = lax.rem(index, BUFS)
         his = []
         los = []
+        tops = []
         for c in range(PARTS):
             x = entries(index * CHUNK, CHUNK, c)
             hi = x.astype(BF16)
             his.append(hi)
-            los.append((x - hi.astype(F32)).astype(BF16))
-        hi = jnp.concatenate(his, axis=1)
-        lo = jnp.concatenate(los, axis=1)
-        update = jnp.dot(hi, slab_hi[...], preferred_element_type=F32)
-        update += jnp.dot(hi, slab_lo[...], preferred_element_type=F32)
-        update += jnp.dot(lo, slab_hi[...], preferred_element_type=F32)
+            los.append(((x - hi.astype(F32)) * 512.0).astype(F8))
+            tops.append(x.astype(F8))
+        update = jnp.dot(jnp.concatenate(los + tops, axis=1), slab_lo[...], preferred_element_type=F32) * shrink
+        update += jnp.dot(jnp.concatenate(his, axis=1), slab_hi[...], preferred_element_type=F32)
         fetch(index, slot).wait()
 
         @pl.when(index >= BUFS)
@@ -462,24 +479,24 @@
             jax.ShapeDtypeStruct((rows, width), F32),
             jax.ShapeDtypeStruct((own,), F32),
         ),
-        in_specs=[smem] + [hbm] * 5 + [vmem, hbm, vmem, vmem, vmem, hbm],
+        in_specs=[smem] + [hbm] * 7 + [vmem, hbm, vmem, vmem, vmem, hbm],
         out_specs=(hbm, vmem),
-        scratch_shapes=[pltpu.SMEM((entries,), I32)] * 4
+        scratch_shapes=[pltpu.SMEM((entries,), I32)] * 6
         + [pltpu.SMEM((entries,), F32)]
         + [
             pltpu.VMEM((RING * SLOT * WIDE, 128), F32),
             pltpu.VMEM((RING * WIDE, 128), F32),
-            pltpu.VMEM((TOP * 4, 8, 128), F32),
-            pltpu.VMEM((TOP * 4, 8, 128), F32),
+            pltpu.VMEM((TOP * 32, 128), F32),
+            pltpu.VMEM((TOP * 32, 128), F32),
             pltpu.VMEM(((rows + width + 1) * PITCH, 128), F32),
             pltpu.VMEM((GROUPS * 64, 128), F32),
             pltpu.VMEM((GROUPS * 64, 128), F32),
             pltpu.VMEM((BLOCKS * 8 + 8, 128), F32),
             pltpu.VMEM((OBS, width), BF16),
-            pltpu.VMEM((OBS, width), BF16),
+            pltpu.VMEM((2 * OBS, width), F8),
             pltpu.VMEM((BUFS, CHUNK, width), F32),
             pltpu.VMEM((BUFS, CHUNK, width), F32),
-            pltpu.SemaphoreType.DMA((6,)),
+            pltpu.SemaphoreType.DMA((8,)),
             pltpu.SemaphoreType.DMA((BUFS,)),
             pltpu.SemaphoreType.DMA((BUFS,)),
         ],
@@ -504,10 +521,10 @@
     vmem = pl.BlockSpec(memory_space=pltpu.VMEM)
     outs = pl.pallas_call(
         gather_kernel,
-        out_shape=tuple(jax.ShapeDtypeStruct(shape, I32) for _ in range(4))
+        out_shape=tuple(jax.ShapeDtypeStruct(shape, I32) for _ in range(6))
         + (jax.ShapeDtypeStruct(shape, F32), jax.ShapeDtypeStruct((64, 128), F32)),
         in_specs=[vmem] * 6 + [pl.BlockSpec(memory_space=pltpu.HBM), vmem],
-        out_specs=(vmem,) * 6,
+        out_specs=(vmem,) * 8,
         scratch_shapes=[
             pltpu.VMEM((8, 128), F32),
             pltpu.VMEM((count, 8, 128), F32),
@@ -520,8 +537,8 @@
         compiler_params=pltpu.CompilerParams(collective_id=0, has_side_effects=True),
         name="gather_observations",
     )(colatitude, longitude, radius_ratio, component, obs_weight, observed, unknown_map, slab_map)
-    facts = tuple(x.reshape(entries) for x in outs[:5])
-    return local_update(outs[5], col, facts, normal_slab, right_side)
+    facts = tuple(x.reshape(entries) for x in outs[:7])
+    return local_update(outs[7], col, facts, normal_slab, right_side)
 
 
 def solution(mesh):

time: 99.7 us -> 87.1 us (0.87)
  Pallas kernels: 98.8 us -> 86.3 us
    pallas_call x1, Pallas kernels: 82.9 us -> 70.2 us  [local_update(): pl.pallas_call(kernel, out_shape=(jax.ShapeDtypeStruct((rows, width), F32...]
where the time goes in v4:
time: 87.1 us; the launch traced here: 86.9 us
  Pallas kernels  86.3 us (99%)
    pallas_call x1, Pallas kernels, local_update(): pl.pallas_call(kernel, out_shape=(jax.ShapeDtypeStruct((rows, width), F32...  70.2 us
    pallas_call x1, Pallas kernels, on_device(): pl.pallas_call(gather_kernel, out_shape=tuple((jax.ShapeDtypeStruct(shape...  16 us

profile of v4, /device:TPU:1, one launch (start us, length us, event | category | flops | bytes accessed | tf_op | source)
XLA Modules:
  0.0 86.9 jit_solution(13714201326875530141)
XLA Ops:
  0.6 16.0 %gather_observations.1 = (s32[56,128]{1,0:T(8,128)}, s32[56,128]{1,0:T(8,128)}, s32[56,128]{1,0:T(8,128)}, s32[56,128]{1,0:T(8,128)}, s32[56,128]{1,0:T(8,128)},...) custom-call(f32[64]{0:T(128)} %theta_ref.1, f32[64]{0:T(128)} %lon_ref.1, f32[64]{0:T(128)} %ratio_ref.1, ...), custom_call_target="tpu_custom_call" | custom-call | tf_op jit(solution)/shard_map/gather_observations/pallas_call | solution.py:522
  16.7 70.2 %normal_update.1 = (f32[6144,512]{1,0:T(8,128)}, f32[768]{0:T(1024)}) custom-call(s32[1]{0:T(128)} %bitcast.col_ref, s32[7168]{0:T(1024)} %bitcast.8, s32[7168]{0:T(1024)} %bitcast.9, s32[7168]{0:T(1024)} %bitcast.10, s32[7168]{0:T(1024)} %bitcast.11, s32[7168]{0:T(1024)} %bitcast.12, s32[7168]{0:T(1024)} %bitcast.13, f32[7168]{0:T(1024)} %bitcast.14, ...), custom_call_target="tpu_custom_call" | custom-call | tf_op jit(solution)/shard_map/normal_update/pallas_call | solution.py:476

commit v5 on v4

--- a/solution.py
+++ b/solution.py
@@ -22,6 +22,7 @@
 PACE = 16
 BATCH = 2
 DRAIN = 16
+BODY = 4
 LATE = 1 << 20
 BIG = float(2.0**64)
 SMALL = float(2.0**-64)
@@ -48,7 +49,7 @@
     for group in range(GROUPS):
         order = (group * GROUP + np.arange(GROUP, dtype=np.float64))[:, None]
         for block in range(blocks_of(group)):
-            sigma = np.ones((GROUP, 1))
+            sigma = np.zeros((GROUP, 1))
             if block > 0:
                 degree = order + STEP * (block - 1) + np.arange(STEP)[None, :]
                 ratio = (degree**2 - order**2) / (degree**2 - 0.25)
@@ -56,7 +57,7 @@
                     ratio[:, 0] = 1.0
                 sigma = 1.0 / np.sqrt(np.prod(ratio, axis=1, keepdims=True))
             table.append(np.broadcast_to(sigma, (GROUP, 128)))
-    table.append(np.ones((GROUP, 128)))
+    table += [np.zeros((GROUP, 128))] * (STEPS - len(table))
     return np.concatenate(table, axis=0).astype(np.float32)
 
 
@@ -66,6 +67,17 @@
 
 
 BLOCKS = sum(blocks_of(group) for group in range(GROUPS))
+STEPS = -(-BLOCKS // BODY) * BODY
+
+
+def block_lists():
+    lists = np.zeros((2, STEPS), np.int32)
+    at = 0
+    for group in range(GROUPS):
+        for block in range(blocks_of(group)):
+            lists[:, at] = group * GROUP, group * GROUP + block * STEP
+            at += 1
+    return lists.reshape(-1)
 
 
 def row_key(degree, order, kind, place):
@@ -196,11 +208,11 @@
 
 
 def kernel(
-    col_ref, number_hbm, value_hbm, scale_hbm, radial_hbm, harm_hbm, target_hbm, grow_hbm,
+    col_ref, blocks_ref, number_hbm, value_hbm, scale_hbm, radial_hbm, harm_hbm, target_hbm, grow_hbm,
     params_ref, table_hbm, inv_ref, logs_ref, right_ref, normal_ref,
     out_ref, right_out_ref,
     number_ref, value_ref, scale_ref, radial_ref, harm_ref, target_ref, grow_ref,
-    value_buf, scale_buf, harm_buf, radial_buf, design_buf, seed_buf, level_buf, table_ref,
+    value_buf, scale_buf, harm_buf, radial_buf, design_buf, seed_buf, level_buf, square_buf, table_ref,
     slab_hi, slab_lo, in_buf, out_buf, list_sem, in_sem, out_sem,
 ):
     rows, width = normal_ref.shape
@@ -294,7 +306,9 @@
             radial_buf[pl.ds(pl.multiple_of(base * 32, 32) + j * 32 + 24, 8), :] = u
         orders = subf + base.astype(F32)
         diag = logs_ref[pl.ds(pl.multiple_of(base, 8), 8), :]
-        before = -1.0 / (1.0 - (orders * orders - 0.25) * inv_ref[pl.ds(pl.multiple_of(base, 8), 8), :])
+        square = orders * orders - 0.25
+        square_buf[pl.ds(pl.multiple_of(base, 8), 8), :] = square
+        before = -1.0 / (1.0 - square * inv_ref[pl.ds(pl.multiple_of(base, 8), 8), :])
         for c in range(PARTS):
             log_seed = diag + orders * logs[c]
             level = jnp.minimum(jnp.ceil(log_seed * (1.0 / LOG_BIG)), 0.0)
@@ -331,64 +345,63 @@
         def piece(at):
             for u in range(DRAIN):
                 make_row(at + u)
-            kept = at + 0
-            for u in range(DRAIN):
-                kept = kept + (number_ref[at + u] <= number).astype(I32)
-            return kept
+            return at + passed(at, number + 1)
 
         return lax.while_loop(more, piece, cursor)
 
-    def group_body(group, carry):
-        cursor, number = carry
-        zero = jnp.zeros((8, 128), F32)
-        orders = subf + (group * GROUP).astype(F32)
-        squares = orders * orders - 0.25
-        at = pl.multiple_of(group * 64, 64)
-        one = tuple(zero for _ in range(PARTS))
-        two = tuple(seed_buf[pl.ds(at + c * 8, 8), :] for c in range(PARTS))
-        levels = tuple(level_buf[pl.ds(at + c * 8, 8), :] for c in range(PARTS))
-
-        def factors(number):
-            sigma = table_ref[pl.ds(pl.multiple_of(number * 8, 8), 8), :]
-            return sigma, sigma * SMALL, 64.0 / sigma
-
-        def block_body(block, carry):
-            one, two, levels, (sigma, sigma_small, limit), cursor, number = carry
-            one, two, levels = list(one), list(two), list(levels)
-            cursor = drain(cursor, number - RING)
-            ring = number & (RING - 1)
-            first = pl.multiple_of(group * GROUP + block * STEP, 8)
-            at_scale = ring * WIDE
-            at_value = ring * (SLOT * WIDE)
+    def passed(at, number):
+        done = jnp.int32(0)
+        for half in (8, 4, 2, 1, 1):
+            done = done + jnp.where(number_ref[at + done + (half - 1)] < number, half, 0)
+        return done
+
+    zero = jnp.zeros((8, 128), F32)
+
+    def block_step(number, state, cursor):
+        one, two, levels = [list(x) for x in state]
+        order = blocks_ref[number]
+        first = blocks_ref[STEPS + number]
+        ring = number & (RING - 1)
+        at_scale = ring * WIDE
+        at_value = ring * (SLOT * WIDE)
+        at_seed = pl.multiple_of(order * 8, 64)
+        opens = jnp.broadcast_to(order == first, (8, 128))
+        sigma = table_ref[pl.ds(pl.multiple_of(number * 8, 8), 8), :]
+        sigma_small = sigma * SMALL
+        limit = 64.0 / sigma
+        squares = square_buf[pl.ds(pl.multiple_of(order, 8), 8), :]
+        for c in range(PARTS):
+            big = jnp.abs(one[c]) > limit
+            factor = jnp.where(big, sigma_small, sigma)
+            one[c] = one[c] * factor
+            two[c] = jnp.where(opens, seed_buf[pl.ds(at_seed + c * 8, 8), :], two[c] * factor)
+            level = levels[c] + jnp.where(big, 64.0, 0.0)
+            levels[c] = jnp.where(opens, level_buf[pl.ds(at_seed + c * 8, 8), :], level)
+            value_buf[pl.ds(at_value + c * PITCH, 8), :] = one[c]
+        for i in range(STEP):
+            if i % BATCH == 0:
+                for k in range(i * PACE // STEP, (i + BATCH) * PACE // STEP):
+                    make_row(cursor + k)
+            rho = 1.0 - squares * inv_ref[pl.ds(first + i, 8), :]
+            fresh = [twice[c] * one[c] - rho * two[c] for c in range(PARTS)]
             for c in range(PARTS):
-                big = jnp.abs(one[c]) > limit
-                factor = jnp.where(big, sigma_small, sigma)
-                one[c] = one[c] * factor
-                two[c] = two[c] * factor
-                levels[c] = levels[c] + jnp.where(big, 64.0, 0.0)
-                value_buf[pl.ds(at_value + c * PITCH, 8), :] = one[c]
-            for i in range(STEP):
-                if i % BATCH == 0:
-                    for k in range(i * PACE // STEP, (i + BATCH) * PACE // STEP):
-                        make_row(cursor + k)
-                rho = 1.0 - squares * inv_ref[pl.ds(first + i, 8), :]
-                fresh = [twice[c] * one[c] - rho * two[c] for c in range(PARTS)]
-                for c in range(PARTS):
-                    value_buf[pl.ds(at_value + (1 + i) * WIDE + c * PITCH, 8), :] = fresh[c]
-                one, two = fresh, one
-            for c in range(PARTS):
-                scale_buf[pl.ds(at_scale + c * PITCH, 8), :] = jnp.exp2(levels[c])
-            done = jnp.int32(0)
-            for half in (8, 4, 2, 1, 1):
-                done = done + jnp.where(number_ref[cursor + done + (half - 1)] < number, half, 0)
-            cursor = cursor + jnp.minimum(done, PACE)
-            return tuple(one), tuple(two), tuple(levels), factors(number + 1), cursor, number + 1
-
-        blocks = (NMAX + STEP - group * GROUP) // STEP
-        out = lax.fori_loop(0, blocks, block_body, (one, two, levels, factors(number), cursor, number))
-        return out[4], out[5]
-
-    cursor, _ = lax.fori_loop(0, GROUPS, group_body, (jnp.int32(0), jnp.int32(0)))
+                value_buf[pl.ds(at_value + (1 + i) * WIDE + c * PITCH, 8), :] = fresh[c]
+            one, two = fresh, one
+        for c in range(PARTS):
+            scale_buf[pl.ds(at_scale + c * PITCH, 8), :] = jnp.exp2(levels[c])
+        return tuple(one), tuple(two), tuple(levels)
+
+    def body(index, carry):
+        state, cursor = carry
+        number = index * BODY
+        cursor = drain(cursor, number + BODY - 1 - RING)
+        for k in range(BODY):
+            state = block_step(number + k, state, cursor)
+            cursor = cursor + passed(cursor, number + k)
+        return state, cursor
+
+    still = tuple((zero,) * PARTS for _ in range(3))
+    _, cursor = lax.fori_loop(0, STEPS // BODY, body, (still, jnp.int32(0)))
     cursor = drain(cursor, BLOCKS)
 
     def clear(piece, _):
@@ -396,7 +409,6 @@
             design_buf[pl.ds(target_ref[cursor + piece * DRAIN + u], 8), :] = zero
         return 0
 
-    zero = jnp.zeros((8, 128), F32)
     lax.fori_loop(0, (rows + width - cursor + DRAIN - 1) // DRAIN, clear, 0)
 
     def entries(first, count, c):
@@ -479,7 +491,7 @@
             jax.ShapeDtypeStruct((rows, width), F32),
             jax.ShapeDtypeStruct((own,), F32),
         ),
-        in_specs=[smem] + [hbm] * 7 + [vmem, hbm, vmem, vmem, vmem, hbm],
+        in_specs=[smem] * 2 + [hbm] * 7 + [vmem, hbm, vmem, vmem, vmem, hbm],
         out_specs=(hbm, vmem),
         scratch_shapes=[pltpu.SMEM((entries,), I32)] * 6
         + [pltpu.SMEM((entries,), F32)]
@@ -491,7 +503,8 @@
             pltpu.VMEM(((rows + width + 1) * PITCH, 128), F32),
             pltpu.VMEM((GROUPS * 64, 128), F32),
             pltpu.VMEM((GROUPS * 64, 128), F32),
-            pltpu.VMEM((BLOCKS * 8 + 8, 128), F32),
+            pltpu.VMEM((TOP, 128), F32),
+            pltpu.VMEM((STEPS * 8, 128), F32),
             pltpu.VMEM((OBS, width), BF16),
             pltpu.VMEM((2 * OBS, width), F8),
             pltpu.VMEM((BUFS, CHUNK, width), F32),
@@ -503,7 +516,7 @@
         compiler_params=pltpu.CompilerParams(vmem_limit_bytes=62 * 1024 * 1024),
         name="normal_update",
     )(
-        col, *facts, params, jnp.asarray(block_scales()), jnp.asarray(inverse_squares()),
+        col, jnp.asarray(block_lists()), *facts, params, jnp.asarray(block_scales()), jnp.asarray(inverse_squares()),
         jnp.asarray(diagonal_logs()), right_side, normal_slab,
     )
 

time: 87.1 us -> 83.7 us (0.961)
  Pallas kernels: 86.3 us -> 82.9 us
    pallas_call x1, Pallas kernels: 70.2 us -> 66.9 us  [local_update(): pl.pallas_call(kernel, out_shape=(jax.ShapeDtypeStruct((rows, width), F32...]
where the time goes in v5:
time: 83.7 us; the launch traced here: 83.5 us
  Pallas kernels  82.9 us (99%)
    pallas_call x1, Pallas kernels, local_update(): pl.pallas_call(kernel, out_shape=(jax.ShapeDtypeStruct((rows, width), F32...  66.9 us
    pallas_call x1, Pallas kernels, on_device(): pl.pallas_call(gather_kernel, out_shape=tuple((jax.ShapeDtypeStruct(shape...  16 us

profile of v5, /device:TPU:1, one launch (start us, length us, event | category | flops | bytes accessed | tf_op | source)
XLA Modules:
  0.0 83.5 jit_solution(7256978432210865866)
XLA Ops:
  0.6 16.0 %gather_observations.1 = (s32[56,128]{1,0:T(8,128)}, s32[56,128]{1,0:T(8,128)}, s32[56,128]{1,0:T(8,128)}, s32[56,128]{1,0:T(8,128)}, s32[56,128]{1,0:T(8,128)},...) custom-call(f32[64]{0:T(128)} %theta_ref.1, f32[64]{0:T(128)} %lon_ref.1, f32[64]{0:T(128)} %ratio_ref.1, ...), custom_call_target="tpu_custom_call" | custom-call | tf_op jit(solution)/shard_map/gather_observations/pallas_call | solution.py:535
  16.7 66.9 %normal_update.1 = (f32[6144,512]{1,0:T(8,128)}, f32[768]{0:T(1024)}) custom-call(s32[1]{0:T(128)} %bitcast.col_ref, s32[760]{0:T(1024)} %constant.12.clone.blocks_ref, s32[7168]{0:T(1024)} %bitcast.8, s32[7168]{0:T(1024)} %bitcast.9, s32[7168]{0:T(1024)} %bitcast.10, s32[7168]{0:T(1024)} %bitcast.11, s32[7168]{0:T(1024)} %bitcast.12, s32[7168]{0:T(1024)} %bitcast.13, ...), custom_call_target="tpu_custom_call" | custom-call | tf_op jit(solution)/shard_map/normal_update/pallas_call | solution.py:488

commit v6 on v5

--- a/solution.py
+++ b/solution.py
@@ -22,8 +22,8 @@
 PACE = 16
 BATCH = 2
 DRAIN = 16
-BODY = 4
-LATE = 1 << 20
+BODY = 5
+LATE = 1 << 14
 BIG = float(2.0**64)
 SMALL = float(2.0**-64)
 LOG_BIG = float(64.0 * np.log(2.0))
@@ -142,13 +142,14 @@
         ratio = (jf * jf - m * m) / (jf * jf - 0.25)
         product = jnp.where((j > order) & (j <= degree), product * ratio, product)
     at_harm = (order * 2 + kind) * 16
-    return number, at_value, at_scale, degree * 32, at_harm, target, lax.rsqrt(product)
+    return (number << 16) | at_scale, (at_value << 16) | at_harm, (degree << 21) | target, lax.rsqrt(product)
 
 
 def gather_kernel(
-    theta_ref, lon_ref, ratio_ref, comp_ref, weight_ref, seen_ref, unknown_ref, slab_ref,
-    number_ref, value_ref, scale_ref, radial_ref, harm_ref, target_ref, grow_ref, params_ref,
-    local, everyone, map_buf, key_buf, send_sem, recv_sem, map_sem,
+    theta_hbm, lon_hbm, ratio_hbm, comp_hbm, weight_hbm, seen_hbm, unknown_ref, slab_hbm,
+    number_ref, value_ref, target_ref, grow_ref, params_ref,
+    theta_ref, lon_ref, ratio_ref, comp_ref, weight_ref, seen_ref, slab_ref,
+    local, everyone, map_buf, key_buf, send_sem, recv_sem, map_sem, in_sem,
 ):
     me = lax.axis_index("row")
     count = everyone.shape[0]
@@ -158,13 +159,31 @@
     read_map = pltpu.make_async_copy(
         unknown_ref.at[:, pl.ds(pl.multiple_of(me * rows, 128), rows)], map_buf, map_sem.at[0]
     )
-    read_map.start()
+    inputs = [
+        pltpu.make_async_copy(src, dst, in_sem.at[k])
+        for k, (src, dst) in enumerate(
+            (
+                (theta_hbm, theta_ref),
+                (lon_hbm, lon_ref),
+                (ratio_hbm, ratio_ref),
+                (comp_hbm, comp_ref),
+                (weight_hbm, weight_ref),
+                (seen_hbm, seen_ref),
+                (slab_hbm, slab_ref),
+            )
+        )
+    ]
     barrier = pltpu.get_barrier_semaphore()
     for d in range(1, count):
         pl.semaphore_signal(
             barrier, inc=1, device_id={"row": lax.rem(me + d, count)}, device_id_type=pl.DeviceIdType.MESH
         )
+    for copy in inputs:
+        copy.start()
+    read_map.start()
     local[...] = jnp.zeros_like(local)
+    for copy in inputs:
+        copy.wait()
     for k, ref in enumerate((theta_ref, lon_ref, ratio_ref, comp_ref, weight_ref, seen_ref)):
         local[pl.ds(k, 1), pl.ds(0, half)] = ref[...].astype(F32).reshape(1, half)
     pl.semaphore_wait(barrier, count - 1)
@@ -194,7 +213,7 @@
     place = lax.broadcasted_iota(I32, key_buf.shape, 0) * 128 + lax.broadcasted_iota(I32, key_buf.shape, 1)
     key = sort_keys(jnp.where(place < rows + width, key_buf[...], (31 << 26) | place))
     facts = list_facts(key[: number_ref.shape[0]], rows + width)
-    outs = (number_ref, value_ref, scale_ref, radial_ref, harm_ref, target_ref, grow_ref)
+    outs = (number_ref, value_ref, target_ref, grow_ref)
     for ref, value in zip(outs, facts):
         ref[...] = value
     for d in range(1, count):
@@ -208,10 +227,10 @@
 
 
 def kernel(
-    col_ref, blocks_ref, number_hbm, value_hbm, scale_hbm, radial_hbm, harm_hbm, target_hbm, grow_hbm,
+    col_ref, blocks_ref, number_hbm, value_hbm, target_hbm, grow_hbm,
     params_ref, table_hbm, inv_ref, logs_ref, right_ref, normal_ref,
     out_ref, right_out_ref,
-    number_ref, value_ref, scale_ref, radial_ref, harm_ref, target_ref, grow_ref,
+    number_ref, value_ref, target_ref, grow_ref,
     value_buf, scale_buf, harm_buf, radial_buf, design_buf, seed_buf, level_buf, square_buf, table_ref,
     slab_hi, slab_lo, in_buf, out_buf, list_sem, in_sem, out_sem,
 ):
@@ -222,14 +241,11 @@
         pltpu.make_async_copy(src, dst, list_sem.at[k])
         for k, (src, dst) in enumerate(
             (
-                (table_hbm, table_ref),
                 (number_hbm, number_ref),
                 (value_hbm, value_ref),
-                (scale_hbm, scale_ref),
-                (radial_hbm, radial_ref),
-                (harm_hbm, harm_ref),
                 (target_hbm, target_ref),
                 (grow_hbm, grow_ref),
+                (table_hbm, table_ref),
             )
         )
     ]
@@ -246,8 +262,6 @@
             out_buf.at[slot], out_ref.at[pl.ds(pl.multiple_of(index * CHUNK, CHUNK), CHUNK)], out_sem.at[slot]
         )
 
-    for k in range(BUFS):
-        fetch(k, k).start()
 
     def param(k):
         return params_ref[pl.ds(8 * k, 8), :]
@@ -325,22 +339,26 @@
 
     for copy in lists:
         copy.wait()
+    for k in range(BUFS):
+        fetch(k, k).start()
 
     def make_row(j):
-        at = value_ref[j]
+        values = value_ref[j]
+        targets = target_ref[j]
+        at = values >> 16
         now = value_buf[pl.ds(at, 8, stride=PITCH), :]
         past = value_buf[pl.ds(at - WIDE, 8, stride=PITCH), :]
-        scale = scale_buf[pl.ds(scale_ref[j], 8, stride=PITCH), :]
-        n = pl.multiple_of(radial_ref[j], 32)
-        h = pl.multiple_of(harm_ref[j], 16)
+        scale = scale_buf[pl.ds(number_ref[j] & 65535, 8, stride=PITCH), :]
+        n = pl.multiple_of(targets >> 16, 32)
+        h = pl.multiple_of(values & 65535, 16)
         kept = now * radial_buf[pl.ds(n, 8), :] - past * radial_buf[pl.ds(n + 16, 8), :]
         spun = now * radial_buf[pl.ds(n + 8, 8), :] - past * radial_buf[pl.ds(n + 24, 8), :]
         body = harm_buf[pl.ds(h, 8), :] * kept - harm_buf[pl.ds(h + 8, 8), :] * spun
-        design_buf[pl.ds(target_ref[j], 8), :] = body * (scale * grow_ref[j])
+        design_buf[pl.ds(targets & 65535, 8), :] = body * (scale * grow_ref[j])
 
     def drain(cursor, number):
         def more(at):
-            return number_ref[at] <= number
+            return number_ref[at] < ((number + 1) << 16)
 
         def piece(at):
             for u in range(DRAIN):
@@ -352,7 +370,7 @@
     def passed(at, number):
         done = jnp.int32(0)
         for half in (8, 4, 2, 1, 1):
-            done = done + jnp.where(number_ref[at + done + (half - 1)] < number, half, 0)
+            done = done + jnp.where(number_ref[at + done + (half - 1)] < (number << 16), half, 0)
         return done
 
     zero = jnp.zeros((8, 128), F32)
@@ -406,7 +424,7 @@
 
     def clear(piece, _):
         for u in range(DRAIN):
-            design_buf[pl.ds(target_ref[cursor + piece * DRAIN + u], 8), :] = zero
+            design_buf[pl.ds(target_ref[cursor + piece * DRAIN + u] & 65535, 8), :] = zero
         return 0
 
     lax.fori_loop(0, (rows + width - cursor + DRAIN - 1) // DRAIN, clear, 0)
@@ -491,9 +509,9 @@
             jax.ShapeDtypeStruct((rows, width), F32),
             jax.ShapeDtypeStruct((own,), F32),
         ),
-        in_specs=[smem] * 2 + [hbm] * 7 + [vmem, hbm, vmem, vmem, vmem, hbm],
+        in_specs=[smem] * 2 + [hbm] * 4 + [vmem, hbm, vmem, vmem, vmem, hbm],
         out_specs=(hbm, vmem),
-        scratch_shapes=[pltpu.SMEM((entries,), I32)] * 6
+        scratch_shapes=[pltpu.SMEM((entries,), I32)] * 3
         + [pltpu.SMEM((entries,), F32)]
         + [
             pltpu.VMEM((RING * SLOT * WIDE, 128), F32),
@@ -509,7 +527,7 @@
             pltpu.VMEM((2 * OBS, width), F8),
             pltpu.VMEM((BUFS, CHUNK, width), F32),
             pltpu.VMEM((BUFS, CHUNK, width), F32),
-            pltpu.SemaphoreType.DMA((8,)),
+            pltpu.SemaphoreType.DMA((5,)),
             pltpu.SemaphoreType.DMA((BUFS,)),
             pltpu.SemaphoreType.DMA((BUFS,)),
         ],
@@ -534,11 +552,18 @@
     vmem = pl.BlockSpec(memory_space=pltpu.VMEM)
     outs = pl.pallas_call(
         gather_kernel,
-        out_shape=tuple(jax.ShapeDtypeStruct(shape, I32) for _ in range(6))
+        out_shape=tuple(jax.ShapeDtypeStruct(shape, I32) for _ in range(3))
         + (jax.ShapeDtypeStruct(shape, F32), jax.ShapeDtypeStruct((64, 128), F32)),
-        in_specs=[vmem] * 6 + [pl.BlockSpec(memory_space=pltpu.HBM), vmem],
-        out_specs=(vmem,) * 8,
+        in_specs=[pl.BlockSpec(memory_space=pltpu.HBM)] * 8,
+        out_specs=(vmem,) * 5,
         scratch_shapes=[
+            pltpu.VMEM(colatitude.shape, F32),
+            pltpu.VMEM(colatitude.shape, F32),
+            pltpu.VMEM(colatitude.shape, F32),
+            pltpu.VMEM(colatitude.shape, I32),
+            pltpu.VMEM(colatitude.shape, F32),
+            pltpu.VMEM(colatitude.shape, F32),
+            pltpu.VMEM(slab_map.shape, I32),
             pltpu.VMEM((8, 128), F32),
             pltpu.VMEM((count, 8, 128), F32),
             pltpu.VMEM((3, rows), I32),
@@ -546,12 +571,13 @@
             pltpu.SemaphoreType.DMA((count,)),
             pltpu.SemaphoreType.DMA((count,)),
             pltpu.SemaphoreType.DMA((1,)),
+            pltpu.SemaphoreType.DMA((7,)),
         ],
         compiler_params=pltpu.CompilerParams(collective_id=0, has_side_effects=True),
         name="gather_observations",
     )(colatitude, longitude, radius_ratio, component, obs_weight, observed, unknown_map, slab_map)
-    facts = tuple(x.reshape(entries) for x in outs[:7])
-    return local_update(outs[7], col, facts, normal_slab, right_side)
+    facts = tuple(x.reshape(entries) for x in outs[:4])
+    return local_update(outs[4], col, facts, normal_slab, right_side)
 
 
 def solution(mesh):

time: 83.7 us -> 82.3 us (0.983)
  Pallas kernels: 82.9 us -> 81.4 us
where the time goes in v6:
time: 82.3 us; the launch traced here: 82 us
  Pallas kernels  81.4 us (99%)
    pallas_call x1, Pallas kernels, local_update(): pl.pallas_call(kernel, out_shape=(jax.ShapeDtypeStruct((rows, width), F32...  66.1 us
    pallas_call x1, Pallas kernels, on_device(): pl.pallas_call(gather_kernel, out_shape=tuple((jax.ShapeDtypeStruct(shape...  15.3 us

profile of v6, /device:TPU:1, one launch (start us, length us, event | category | flops | bytes accessed | tf_op | source)
XLA Modules:
  0.0 82.0 jit_solution(4895591263471148237)
XLA Ops:
  0.6 15.3 %gather_observations.1 = (s32[56,128]{1,0:T(8,128)}, s32[56,128]{1,0:T(8,128)}, s32[56,128]{1,0:T(8,128)}, f32[56,128]{1,0:T(8,128)}, f32[64,128]{1,0:T(8,128)}) custom-call(f32[64]{0:T(128)} %theta_hbm.1, f32[64]{0:T(128)} %lon_hbm.1, f32[64]{0:T(128)} %ratio_hbm.1, s32[64]{0:T(128)} %comp_hbm.1, f32[64]{0:T(128)} %weight_hbm.1, f32[64]{0:T(128)} %seen_hbm.1, ...), custom_call_target="tpu_custom_call" | custom-call | tf_op jit(solution)/shard_map/gather_observations/pallas_call | solution.py:553
  15.9 66.1 %normal_update.1 = (f32[6144,512]{1,0:T(8,128)}, f32[768]{0:T(1024)}) custom-call(s32[1]{0:T(128)} %bitcast.col_ref, s32[760]{0:T(1024)} %constant.12.clone.blocks_ref, s32[7168]{0:T(1024)} %bitcast.5, s32[7168]{0:T(1024)} %bitcast.6, s32[7168]{0:T(1024)} %bitcast.7, f32[7168]{0:T(1024)} %bitcast.8, f32[64,128]{1,0:T(8,128)} %get-tuple-element.11.params_ref, ...), custom_call_target="tpu_custom_call" | custom-call | tf_op jit(solution)/shard_map/normal_update/pallas_call | solution.py:506

commit v7 on v6

--- a/solution.py
+++ b/solution.py
@@ -93,27 +93,29 @@
     return jnp.where(kind == 2, (31 << 26) | place, key)
 
 
-def sort_keys(key):
+def sort_keys(key, turn):
     height = key.shape[0]
     total = height * 128
     row = lax.broadcasted_iota(I32, key.shape, 0)
     lane = lax.broadcasted_iota(I32, key.shape, 1)
-    index = row * 128 + lane
+    index = lane * height + row
     size = 2
     while size <= total:
         rising = (index & size) == 0
         stride = size // 2
         while stride >= 1:
             low = (index & stride) == 0
-            if stride < 128:
-                ahead, behind = pltpu.roll(key, 128 - stride, 1), pltpu.roll(key, stride, 1)
+            if stride < height:
+                ahead, behind = pltpu.roll(key, height - stride, 0), pltpu.roll(key, stride, 0)
             else:
-                ahead, behind = pltpu.roll(key, height - stride // 128, 0), pltpu.roll(key, stride // 128, 0)
+                ahead, behind = pltpu.roll(key, 128 - stride // height, 1), pltpu.roll(key, stride // height, 1)
             other = jnp.where(low, ahead, behind)
             key = jnp.where(low == rising, jnp.minimum(key, other), jnp.maximum(key, other))
             stride //= 2
         size *= 2
-    return key
+    columns = key.T
+    turn[...] = jnp.concatenate([columns, columns], axis=1)
+    return jnp.where(lane < height, turn[pl.ds(0, height, stride=2), :], turn[pl.ds(1, height, stride=2), :])
 
 
 def list_facts(key, limit):
@@ -149,7 +151,7 @@
     theta_hbm, lon_hbm, ratio_hbm, comp_hbm, weight_hbm, seen_hbm, unknown_ref, slab_hbm,
     number_ref, value_ref, target_ref, grow_ref, params_ref,
     theta_ref, lon_ref, ratio_ref, comp_ref, weight_ref, seen_ref, slab_ref,
-    local, everyone, map_buf, key_buf, send_sem, recv_sem, map_sem, in_sem,
+    local, everyone, map_buf, key_buf, turn, send_sem, recv_sem, map_sem, in_sem,
 ):
     me = lax.axis_index("row")
     count = everyone.shape[0]
@@ -211,7 +213,7 @@
         part = [ref[pl.ds(k, 1), pl.ds(at, 128)] for k in range(3)]
         key_buf[pl.ds(t, 1), :] = row_key(part[0], part[1], part[2], lanes + t * 128)
     place = lax.broadcasted_iota(I32, key_buf.shape, 0) * 128 + lax.broadcasted_iota(I32, key_buf.shape, 1)
-    key = sort_keys(jnp.where(place < rows + width, key_buf[...], (31 << 26) | place))
+    key = sort_keys(jnp.where(place < rows + width, key_buf[...], (31 << 26) | place), turn)
     facts = list_facts(key[: number_ref.shape[0]], rows + width)
     outs = (number_ref, value_ref, target_ref, grow_ref)
     for ref, value in zip(outs, facts):
@@ -568,6 +570,7 @@
             pltpu.VMEM((count, 8, 128), F32),
             pltpu.VMEM((3, rows), I32),
             pltpu.VMEM((total // 128, 128), I32),
+            pltpu.VMEM((128, 128), I32),
             pltpu.SemaphoreType.DMA((count,)),
             pltpu.SemaphoreType.DMA((count,)),
             pltpu.SemaphoreType.DMA((1,)),

time: 82.3 us -> 79.2 us (0.962)
  Pallas kernels: 81.4 us -> 78.3 us
    pallas_call x1, Pallas kernels: 15.3 us -> 12.6 us  [on_device(): pl.pallas_call(gather_kernel, out_shape=tuple((jax.ShapeDtypeStruct(shape...]
where the time goes in v7:
time: 79.2 us; the launch traced here: 78.9 us
  Pallas kernels  78.3 us (99%)
    pallas_call x1, Pallas kernels, local_update(): pl.pallas_call(kernel, out_shape=(jax.ShapeDtypeStruct((rows, width), F32...  65.7 us
    pallas_call x1, Pallas kernels, on_device(): pl.pallas_call(gather_kernel, out_shape=tuple((jax.ShapeDtypeStruct(shape...  12.6 us

profile of v7, /device:TPU:1, one launch (start us, length us, event | category | flops | bytes accessed | tf_op | source)
XLA Modules:
  0.0 78.9 jit_solution(4987510920413982388)
XLA Ops:
  0.6 12.6 %gather_observations.1 = (s32[56,128]{1,0:T(8,128)}, s32[56,128]{1,0:T(8,128)}, s32[56,128]{1,0:T(8,128)}, f32[56,128]{1,0:T(8,128)}, f32[64,128]{1,0:T(8,128)}) custom-call(f32[64]{0:T(128)} %theta_hbm.1, f32[64]{0:T(128)} %lon_hbm.1, f32[64]{0:T(128)} %ratio_hbm.1, s32[64]{0:T(128)} %comp_hbm.1, f32[64]{0:T(128)} %weight_hbm.1, f32[64]{0:T(128)} %seen_hbm.1, ...), custom_call_target="tpu_custom_call" | custom-call | tf_op jit(solution)/shard_map/gather_observations/pallas_call | solution.py:555
  13.2 65.7 %normal_update.1 = (f32[6144,512]{1,0:T(8,128)}, f32[768]{0:T(1024)}) custom-call(s32[1]{0:T(128)} %bitcast.col_ref, s32[760]{0:T(1024)} %constant.12.clone.blocks_ref, s32[7168]{0:T(1024)} %bitcast.5, s32[7168]{0:T(1024)} %bitcast.6, s32[7168]{0:T(1024)} %bitcast.7, f32[7168]{0:T(1024)} %bitcast.8, f32[64,128]{1,0:T(8,128)} %get-tuple-element.11.params_ref, ...), custom_call_target="tpu_custom_call" | custom-call | tf_op jit(solution)/shard_map/normal_update/pallas_call | solution.py:508

commit v8 on v7

--- a/solution.py
+++ b/solution.py
@@ -203,7 +203,7 @@
             device_id={"row": lax.rem(me + d, count)}, device_id_type=pl.DeviceIdType.MESH,
         )
 
-    for d in range(1, count):
+    for d in sorted(range(1, count), key=lambda d: abs(2 * d - count)):
         send(d).start()
     everyone[me] = local[...]
     read_map.wait()

time: 79.2 us -> 79.6 us (level)
  no operation moved by 1% of the time
where the time goes in v8:
time: 79.6 us
  Pallas kernels  78.9 us (99%)
    pallas_call x1, Pallas kernels, local_update(): pl.pallas_call(kernel, out_shape=(jax.ShapeDtypeStruct((rows, width), F32...  66.3 us
    pallas_call x1, Pallas kernels, on_device(): pl.pallas_call(gather_kernel, out_shape=tuple((jax.ShapeDtypeStruct(shape...  12.6 us

profile of v8, /device:TPU:1, one launch (start us, length us, event | category | flops | bytes accessed | tf_op | source)
XLA Modules:
  0.0 79.6 jit_solution(1524529133960004971)
XLA Ops:
  0.6 12.6 %gather_observations.1 = (s32[56,128]{1,0:T(8,128)}, s32[56,128]{1,0:T(8,128)}, s32[56,128]{1,0:T(8,128)}, f32[56,128]{1,0:T(8,128)}, f32[64,128]{1,0:T(8,128)}) custom-call(f32[64]{0:T(128)} %theta_hbm.1, f32[64]{0:T(128)} %lon_hbm.1, f32[64]{0:T(128)} %ratio_hbm.1, s32[64]{0:T(128)} %comp_hbm.1, f32[64]{0:T(128)} %weight_hbm.1, f32[64]{0:T(128)} %seen_hbm.1, ...), custom_call_target="tpu_custom_call" | custom-call | tf_op jit(solution)/shard_map/gather_observations/pallas_call | solution.py:555
  13.3 66.3 %normal_update.1 = (f32[6144,512]{1,0:T(8,128)}, f32[768]{0:T(1024)}) custom-call(s32[1]{0:T(128)} %bitcast.col_ref, s32[760]{0:T(1024)} %constant.12.clone.blocks_ref, s32[7168]{0:T(1024)} %bitcast.5, s32[7168]{0:T(1024)} %bitcast.6, s32[7168]{0:T(1024)} %bitcast.7, f32[7168]{0:T(1024)} %bitcast.8, f32[64,128]{1,0:T(8,128)} %get-tuple-element.11.params_ref, ...), custom_call_target="tpu_custom_call" | custom-call | tf_op jit(solution)/shard_map/normal_update/pallas_call | solution.py:508
